TPU v7x, 256 devices: a whole 4x4x8 slice. The times are simulated.
256 devices in a mesh: seq: 32 (over x, y, core), tp: 8 (over z).
Axes of the slice: x: 4, y: 4, z: 8, core: 2. Of those that a mesh axis runs over, the one named last changes fastest.
Arguments:
- teacher_query: bfloat16 [8192, 8192], P('seq', 'tp'), may hold values from -30 to 30
- teacher_key: bfloat16 [8192, 1024], P('seq', 'tp'), may hold values from -30 to 30
- teacher_value: bfloat16 [8192, 1024], P('seq', 'tp'), may hold values from -192 to 192
- t_segment: int32 [8192], P('seq'), may hold values from 0 to 2, never falling along the last dimension, each value on 1 to 6144 neighbouring positions
- s_hidden: bfloat16 [8192, 3584], P('seq'), may hold values from -80 to 80
- norm_gain: float32 [3584], replicated, may hold values from 0.5 to 1.5
- proj_weight: bfloat16 [3584, 8192], P('seq', 'tp'), may hold values from -0.09375 to 0.09375
- span_start: int32 [8192], P('seq'), may hold values from 0 to 8186, as said below
- span_count: int32 [8192], P('seq'), may hold values from 1 to 6
Outputs:
- grad_proj: float32 [3584, 8192], P('seq', 'tp')
- grad_hidden: float32 [8192, 3584], P('seq', 'tp')
Inputs may be any that keep to these rules, and one draw needn't show every extreme that they name: For student token j, span_start[j] lies within 66 of j.
All inputs are finite; a program needn't handle non-finite values.
Results may differ from a plain program's by a relative error of at most 0.02.
Values may be sent and summed in bfloat16 or wider, within the bound.
A program may use at most 64 MiB of HBM per device.

v0:
```python
import math

import jax
import jax.numpy as jnp
from jax import lax
from jax.sharding import PartitionSpec as P

HEAD_SIZE = 128


def extended(array, sides, width):
    for axis, dim in sides:
        size, length = (lax.axis_size(axis), array.shape[dim])
        up = [(i, (i + 1) % size) for i in range(size - 1)]
        down = [(j, i) for i, j in up]
        last = lax.slice_in_dim(array, length - width, length, axis=dim)
        first = lax.slice_in_dim(array, 0, width, axis=dim)
        before = lax.ppermute(last, axis, up)
        after = lax.ppermute(first, axis, down)
        array = jnp.concatenate([before, array, after], axis=dim)
    return array


def body(
    teacher_query,
    teacher_key,
    teacher_value,
    t_segment,
    s_hidden,
    norm_gain,
    proj_weight,
    span_start,
    span_count,
):
    local_rows = teacher_query.shape[0]
    heads_here = teacher_query.shape[1] // HEAD_SIZE
    pairs_here = teacher_key.shape[1] // HEAD_SIZE
    head_groups = heads_here // pairs_here
    queries = teacher_query.reshape(local_rows, pairs_here, head_groups, HEAD_SIZE)
    first = lax.axis_index("seq") * local_rows
    query_pos = first + jnp.arange(local_rows, dtype=jnp.int32)
    scale = 1.0 / math.sqrt(HEAD_SIZE)

    def attend_block(carry, key_piece, value_piece, doc_piece, start):
        highest, totals, numer = carry
        count = key_piece.shape[0]
        keys_here = key_piece.reshape(count, pairs_here, HEAD_SIZE)
        values_here = value_piece.reshape(count, pairs_here, HEAD_SIZE)
        scores = (
            jnp.einsum("qhgd,khd->hgqk", queries, keys_here, preferred_element_type=jnp.float32)
            * scale
        )
        key_pos = start + jnp.arange(count, dtype=jnp.int32)
        allowed = (t_segment[:, None] == doc_piece.astype(jnp.int32)[None, :]) & (
            key_pos[None, :] <= query_pos[:, None]
        )
        scores = jnp.where(allowed, scores, -1e30)
        new_high = jnp.maximum(highest, jnp.max(scores, axis=-1))
        weights = jnp.where(allowed, jnp.exp(scores - new_high[..., None]), 0.0)
        factor = jnp.exp(highest - new_high)
        totals = totals * factor + jnp.sum(weights, axis=-1)
        update = jnp.einsum(
            "hgqk,khd->hgqd",
            weights.astype(jnp.bfloat16),
            values_here,
            preferred_element_type=jnp.float32,
        )
        numer = numer * factor[..., None] + update
        return (new_high, totals, numer)

    start_high = jnp.full((pairs_here, head_groups, local_rows), -1e30, jnp.float32)
    start_totals = jnp.zeros((pairs_here, head_groups, local_rows), jnp.float32)
    start_numer = jnp.zeros((pairs_here, head_groups, local_rows, HEAD_SIZE), jnp.float32)
    doc_wire = t_segment.astype(jnp.bfloat16)
    carry = (start_high, start_totals, start_numer)
    key_piece = lax.all_gather(teacher_key, "seq", axis=0, tiled=True)
    value_piece = lax.all_gather(teacher_value, "seq", axis=0, tiled=True)
    doc_piece = lax.all_gather(doc_wire, "seq", axis=0, tiled=True)
    count = key_piece.shape[0]
    current_block = math.gcd(count, 512)
    block_count = count // current_block
    key_blocks = key_piece.reshape(block_count, current_block, key_piece.shape[1])
    value_blocks = value_piece.reshape(block_count, current_block, value_piece.shape[1])
    doc_blocks = doc_piece.reshape(block_count, current_block)
    offsets = jnp.arange(block_count, dtype=jnp.int32) * current_block

    def one_block(state, packed):
        key_block, value_block, doc_block, offset = packed
        return (attend_block(state, key_block, value_block, doc_block, offset), None)

    carry, unused = lax.scan(one_block, carry, (key_blocks, value_blocks, doc_blocks, offsets))
    highest, totals, numer = carry
    teacher_out = (
        jnp.transpose(numer / totals[..., None], (2, 0, 1, 3))
        .reshape(local_rows, heads_here * HEAD_SIZE)
        .astype(jnp.bfloat16)
    )
    teacher_rows = extended(teacher_out, (("seq", 0),), local_rows)
    start_index = first - local_rows
    row_ids = start_index + jnp.arange(teacher_rows.shape[0], dtype=jnp.int32)
    span_stop = span_start + span_count
    select = (
        (row_ids[None, :] >= span_start[:, None]) & (row_ids[None, :] < span_stop[:, None])
    ).astype(jnp.bfloat16)
    target = (
        jnp.dot(select, teacher_rows, preferred_element_type=jnp.float32)
        / span_count.astype(jnp.float32)[:, None]
    )
    hidden = s_hidden.astype(jnp.float32)
    width = hidden.shape[1]
    inverse_scale = lax.rsqrt(jnp.mean(hidden * hidden, axis=1, keepdims=True) + 1e-06)
    normed = (hidden * inverse_scale * norm_gain).astype(jnp.bfloat16)
    whole_weight = lax.all_gather(proj_weight, "seq", axis=0, tiled=True)
    prediction = jnp.dot(normed, whole_weight, preferred_element_type=jnp.float32)
    residual_grad = (prediction - target).astype(jnp.bfloat16)
    grad_proj = lax.psum_scatter(
        lax.dot_general(
            normed, residual_grad, (((0,), (0,)), ((), ())), preferred_element_type=jnp.float32
        ).astype(jnp.bfloat16),
        "seq",
        scatter_dimension=0,
        tiled=True,
    ).astype(jnp.float32)
    normed_grad = lax.dot_general(
        residual_grad, whole_weight, (((1,), (1,)), ((), ())), preferred_element_type=jnp.float32
    )
    share = width // lax.axis_size("tp")
    offset = lax.axis_index("tp") * share
    summed_grad = lax.psum(normed_grad.astype(jnp.bfloat16), "tp").astype(jnp.float32)
    scaled = summed_grad * norm_gain
    inner = jnp.sum(scaled * hidden, axis=1, keepdims=True)
    grad_full = inverse_scale * scaled - hidden * inverse_scale**3 * (inner / width)
    grad_hidden = lax.dynamic_slice_in_dim(grad_full, offset, share, 1)
    return (grad_proj, grad_hidden)


def solution(mesh):
    return jax.shard_map(
        body,
        mesh=mesh,
        in_specs=(
            P("seq", "tp"),
            P("seq", "tp"),
            P("seq", "tp"),
            P("seq"),
            P("seq", None),
            P(),
            P("seq", "tp"),
            P("seq"),
            P("seq"),
        ),
        out_specs=(P("seq", "tp"), P("seq", "tp")),
        check_vma=False,
    )
```

profile of v0, /device:TPU:32, one launch (start us, length us, event | category | flops | bytes accessed | tf_op | source)
XLA Modules:
  0.0 534.9 jit_solution(14431326522579430984)
XLA Ops:
  12.3 24.4 %all-gather = bf16[32,1,256]{2,1,0:T(2,128)(2,1)S(1)} all-gather(bf16[1,1,256]{2,1,0:T(2,128)(2,1)S(1)} %reshape.88), channel_id=1, replica_groups=mesh['seq'=32,'tp'=8] {'seq'}, dimensions={0}, use_global_device_ids=true | all-gather | bytes 16896 | tf_op jit(solution)/shard_map/all_gather | solution.py:78
  39.6 22.5 %all-gather.7.cloned.1.call-done = bf16[8192,128]{1,0:T(8,128)(2,1)} async-done(((bf16[256,128]{1,0:T(8,128)(2,1)}), bf16[8192,128]{1,0:T(8,128)(2,1)}) %all-gather.7.cloned.1.call-update) | async-done | bytes 2097168 | tf_op jit(solution)/shard_map/all_gather | solution.py:76
  62.1 50.7 %all-gather.9.cloned.1.call-done = bf16[8192,128]{1,0:T(8,128)(2,1)} async-done(((bf16[256,128]{1,0:T(8,128)(2,1)}), bf16[8192,128]{1,0:T(8,128)(2,1)}) %all-gather.9.cloned.1.call-update) | async-done | bytes 2097168 | tf_op jit(solution)/shard_map/all_gather | solution.py:77
  112.8 208.7 %while.15 = (s32[]{:T(128)}, f32[1,8,256]{2,1,0:T(8,128)S(1)}, f32[1,8,256]{2,1,0:T(8,128)}, f32[1,8,256,128]{3,2,1,0:T(8,128)}, s32[256]{0:T(256)}, /*index=5*/...) while((s32[]{:T(128)}, f32[1,8,256]{2,1,0:T(8,128)S(1)}, ...), condition=%wide.region_4.5_spmd.clone, body=%wide.region_1.4_spmd.clone.sunk | while | flops 551695616 | bytes 41366828 | solution.py:91
  112.8 1.4 dynamic_slice.51
  116.4 3.7 fusion.58
  120.2 4.0 fusion.61
  125.8 1.4 dynamic_slice.51
  129.4 3.7 fusion.58
  133.2 4.0 fusion.61
  138.9 1.4 dynamic_slice.51
  142.4 3.7 fusion.58
  146.2 4.0 fusion.61
  151.9 1.4 dynamic_slice.51
  155.5 3.8 fusion.58
  159.3 4.1 fusion.61
  165.1 1.4 dynamic_slice.51
  168.7 3.8 fusion.58
  172.5 4.0 fusion.61
  178.1 1.4 dynamic_slice.51
  181.7 3.7 fusion.58
  185.5 4.0 fusion.61
  191.2 1.4 dynamic_slice.51
  194.8 3.7 fusion.58
  198.5 4.0 fusion.61
  204.2 1.4 dynamic_slice.51
  207.8 3.7 fusion.58
  211.6 4.0 fusion.61
  217.2 1.4 dynamic_slice.51
  220.8 3.7 fusion.58
  224.6 4.0 fusion.61
  230.3 1.4 dynamic_slice.51
  233.9 3.7 fusion.58
  237.6 4.0 fusion.61
  243.3 1.4 dynamic_slice.51
  246.9 3.7 fusion.58
  250.7 4.0 fusion.61
  256.3 1.4 dynamic_slice.51
  259.9 3.7 fusion.58
  263.7 4.0 fusion.61
  269.4 1.4 dynamic_slice.51
  273.0 3.7 fusion.58
  276.7 4.0 fusion.61
  282.4 1.4 dynamic_slice.51
  286.0 3.7 fusion.58
  289.8 4.0 fusion.61
  295.4 1.4 dynamic_slice.51
  299.0 3.7 fusion.58
  302.8 4.0 fusion.61
  312.0 3.7 fusion.58
  315.8 4.0 fusion.61
  321.5 1.6 copy.26
  323.9 2.1 collective-permute-start
  327.4 5.2 fusion.40
  333.5 2.0 subtract_convert_fusion
  335.5 1.4 copy-done.15
  336.9 3.3 convolution_convert_fusion.1
  340.5 5.2 convolution_convert_fusion
  345.7 2.3 convert_element_type.42
  348.0 79.0 %all-reduce.2.cloned.1.call-done = bf16[256,3584]{1,0:T(8,128)(2,1)} async-done(((bf16[256,3584]{1,0:T(8,128)(2,1)}), bf16[256,3584]{1,0:T(8,128)(2,1)}) %all-reduce.2.cloned.1.call-update) | async-done | bytes 1835024 | tf_op jit(solution)/shard_map/psum | solution.py:129
  427.0 2.2 multiply_reduce_fusion
  429.2 1.6 fusion.38
  431.8 94.9 %reduce-scatter.2.cloned.1.call-done = bf16[112,1024]{1,0:T(8,128)(2,1)} async-done(((bf16[3584,1024]{1,0:T(8,128)(2,1)}), bf16[112,1024]{1,0:T(8,128)(2,1)}) %reduce-scatter.2.cloned.1.call-update) | async-done | bytes 229392 | tf_op jit(solution)/shard_map/reduce_scatter | solution.py:116
  526.6 1.7 convert_element_type.51
  (343 shorter events, 75.2 us)
Async XLA Ops:
  7.2 30.2 %copy-start.1 = (bf16[256,3584]{1,0:T(8,128)(2,1)S(1)}, bf16[256,3584]{1,0:T(8,128)(2,1)}, u32[]{:S(2)}) copy-start(bf16[256,3584]{1,0:T(8,128)(2,1)} %param.15) | copy-start | bytes 5505028
  7.2 31.9 %copy-start.11 = (s32[256]{0:T(256)S(1)}, s32[256]{0:T(256)}, u32[]{:S(2)}) copy-start(s32[256]{0:T(256)} %param.18) | copy-start | bytes 3076
  7.2 31.9 %copy-start.10 = (s32[256]{0:T(256)S(1)}, s32[256]{0:T(256)}, u32[]{:S(2)}) copy-start(s32[256]{0:T(256)} %param.19) | copy-start | bytes 3076
  7.2 54.9 %all-gather.7.cloned.1.call-start = ((), (), s32[]{:S(2)}) async-start(), calls=%async_computation.2 | async-start | bytes 2162688 | tf_op jit(solution)/shard_map/all_gather | solution.py:76
  7.9 104.9 %all-gather.9.cloned.1.call-start = ((), (), s32[]{:S(2)}) async-start(), calls=%async_computation.3 | async-start | bytes 2162688 | tf_op jit(solution)/shard_map/all_gather | solution.py:77
  8.7 318.6 %all-gather.5.cloned.1.call-start = ((), (), s32[]{:S(2)}) async-start(), calls=%async_computation.1 | async-start | bytes 7569408 | tf_op jit(solution)/shard_map/all_gather | solution.py:113
  9.4 417.6 %all-reduce.2.cloned.1.call-start = ((), (), s32[]{:S(2)}) async-start(), calls=%async_computation.5 | async-start | bytes 3670016 | tf_op jit(solution)/shard_map/psum | solution.py:129
  112.8 7.4 %copy-start.2 = (f32[1,8,256,128]{3,2,1,0:T(8,128)S(1)}, f32[1,8,256,128]{3,2,1,0:T(8,128)}, u32[]{:S(2)}) copy-start(f32[1,8,256,128]{3,2,1,0:T(8,128)} %get-tuple-element.265) | copy-start | bytes 3145732 | tf_op jit(solution)/shard_map/while
  120.1 4.0 copy-start
  124.1 1.1 copy-start.3
  125.8 7.4 %copy-start.2 = (f32[1,8,256,128]{3,2,1,0:T(8,128)S(1)}, f32[1,8,256,128]{3,2,1,0:T(8,128)}, u32[]{:S(2)}) copy-start(f32[1,8,256,128]{3,2,1,0:T(8,128)} %get-tuple-element.265) | copy-start | bytes 3145732 | tf_op jit(solution)/shard_map/while
  133.2 4.0 copy-start
  137.2 1.1 copy-start.3
  138.9 7.4 %copy-start.2 = (f32[1,8,256,128]{3,2,1,0:T(8,128)S(1)}, f32[1,8,256,128]{3,2,1,0:T(8,128)}, u32[]{:S(2)}) copy-start(f32[1,8,256,128]{3,2,1,0:T(8,128)} %get-tuple-element.265) | copy-start | bytes 3145732 | tf_op jit(solution)/shard_map/while
  146.2 4.0 copy-start
  150.2 1.1 copy-start.3
  151.9 7.4 %copy-start.2 = (f32[1,8,256,128]{3,2,1,0:T(8,128)S(1)}, f32[1,8,256,128]{3,2,1,0:T(8,128)}, u32[]{:S(2)}) copy-start(f32[1,8,256,128]{3,2,1,0:T(8,128)} %get-tuple-element.265) | copy-start | bytes 3145732 | tf_op jit(solution)/shard_map/while
  159.3 4.1 copy-start
  163.4 1.1 copy-start.3
  165.1 7.4 %copy-start.2 = (f32[1,8,256,128]{3,2,1,0:T(8,128)S(1)}, f32[1,8,256,128]{3,2,1,0:T(8,128)}, u32[]{:S(2)}) copy-start(f32[1,8,256,128]{3,2,1,0:T(8,128)} %get-tuple-element.265) | copy-start | bytes 3145732 | tf_op jit(solution)/shard_map/while
  172.5 4.0 copy-start
  176.5 1.1 copy-start.3
  178.1 7.4 %copy-start.2 = (f32[1,8,256,128]{3,2,1,0:T(8,128)S(1)}, f32[1,8,256,128]{3,2,1,0:T(8,128)}, u32[]{:S(2)}) copy-start(f32[1,8,256,128]{3,2,1,0:T(8,128)} %get-tuple-element.265) | copy-start | bytes 3145732 | tf_op jit(solution)/shard_map/while
  185.5 4.0 copy-start
  189.5 1.1 copy-start.3
  191.2 7.4 %copy-start.2 = (f32[1,8,256,128]{3,2,1,0:T(8,128)S(1)}, f32[1,8,256,128]{3,2,1,0:T(8,128)}, u32[]{:S(2)}) copy-start(f32[1,8,256,128]{3,2,1,0:T(8,128)} %get-tuple-element.265) | copy-start | bytes 3145732 | tf_op jit(solution)/shard_map/while
  198.5 4.0 copy-start
  202.5 1.1 copy-start.3
  204.2 7.3 %copy-start.2 = (f32[1,8,256,128]{3,2,1,0:T(8,128)S(1)}, f32[1,8,256,128]{3,2,1,0:T(8,128)}, u32[]{:S(2)}) copy-start(f32[1,8,256,128]{3,2,1,0:T(8,128)} %get-tuple-element.265) | copy-start | bytes 3145732 | tf_op jit(solution)/shard_map/while
  211.6 4.0 copy-start
  215.6 1.1 copy-start.3
  217.2 7.4 %copy-start.2 = (f32[1,8,256,128]{3,2,1,0:T(8,128)S(1)}, f32[1,8,256,128]{3,2,1,0:T(8,128)}, u32[]{:S(2)}) copy-start(f32[1,8,256,128]{3,2,1,0:T(8,128)} %get-tuple-element.265) | copy-start | bytes 3145732 | tf_op jit(solution)/shard_map/while
  224.6 4.0 copy-start
  228.6 1.1 copy-start.3
  230.3 7.4 %copy-start.2 = (f32[1,8,256,128]{3,2,1,0:T(8,128)S(1)}, f32[1,8,256,128]{3,2,1,0:T(8,128)}, u32[]{:S(2)}) copy-start(f32[1,8,256,128]{3,2,1,0:T(8,128)} %get-tuple-element.265) | copy-start | bytes 3145732 | tf_op jit(solution)/shard_map/while
  237.6 4.0 copy-start
  241.6 1.1 copy-start.3
  243.3 7.3 %copy-start.2 = (f32[1,8,256,128]{3,2,1,0:T(8,128)S(1)}, f32[1,8,256,128]{3,2,1,0:T(8,128)}, u32[]{:S(2)}) copy-start(f32[1,8,256,128]{3,2,1,0:T(8,128)} %get-tuple-element.265) | copy-start | bytes 3145732 | tf_op jit(solution)/shard_map/while
  250.7 4.0 copy-start
  254.6 1.1 copy-start.3
  256.3 7.4 %copy-start.2 = (f32[1,8,256,128]{3,2,1,0:T(8,128)S(1)}, f32[1,8,256,128]{3,2,1,0:T(8,128)}, u32[]{:S(2)}) copy-start(f32[1,8,256,128]{3,2,1,0:T(8,128)} %get-tuple-element.265) | copy-start | bytes 3145732 | tf_op jit(solution)/shard_map/while
  263.7 4.0 copy-start
  269.4 7.4 %copy-start.2 = (f32[1,8,256,128]{3,2,1,0:T(8,128)S(1)}, f32[1,8,256,128]{3,2,1,0:T(8,128)}, u32[]{:S(2)}) copy-start(f32[1,8,256,128]{3,2,1,0:T(8,128)} %get-tuple-element.265) | copy-start | bytes 3145732 | tf_op jit(solution)/shard_map/while
  276.7 4.0 copy-start
  280.7 1.1 copy-start.3
  282.4 7.3 %copy-start.2 = (f32[1,8,256,128]{3,2,1,0:T(8,128)S(1)}, f32[1,8,256,128]{3,2,1,0:T(8,128)}, u32[]{:S(2)}) copy-start(f32[1,8,256,128]{3,2,1,0:T(8,128)} %get-tuple-element.265) | copy-start | bytes 3145732 | tf_op jit(solution)/shard_map/while
  289.7 4.0 copy-start
  293.7 1.1 copy-start.3
  295.4 7.4 %copy-start.2 = (f32[1,8,256,128]{3,2,1,0:T(8,128)S(1)}, f32[1,8,256,128]{3,2,1,0:T(8,128)}, u32[]{:S(2)}) copy-start(f32[1,8,256,128]{3,2,1,0:T(8,128)} %get-tuple-element.265) | copy-start | bytes 3145732 | tf_op jit(solution)/shard_map/while
  302.8 4.0 copy-start
  306.8 1.1 copy-start.3
  308.5 7.4 %copy-start.2 = (f32[1,8,256,128]{3,2,1,0:T(8,128)S(1)}, f32[1,8,256,128]{3,2,1,0:T(8,128)}, u32[]{:S(2)}) copy-start(f32[1,8,256,128]{3,2,1,0:T(8,128)} %get-tuple-element.265) | copy-start | bytes 3145732 | tf_op jit(solution)/shard_map/while
  315.8 4.0 copy-start
  321.5 5.8 %copy-start.6 = (f32[3584]{0:T(1024)S(1)}, f32[3584]{0:T(1024)}, u32[]{:S(2)}) copy-start(f32[3584]{0:T(1024)} %param.16) | copy-start | bytes 43012
  321.5 5.9 %copy-start.7 = (f32[256]{0:T(256)S(1)}, f32[256]{0:T(256)}, u32[]{:S(2)}) copy-start(f32[256]{0:T(256)} %get-tuple-element.171) | copy-start | bytes 3076
  323.9 8.7 %collective-permute-start = (bf16[256,1024]{0,1:T(8,128)(2,1)S(1)}, bf16[256,1024]{0,1:T(8,128)(2,1)S(1)}, u32[]{:S(2)}, u32[]{:S(2)}) collective-permute-start(bf16[256,1024]{0,1:T(8,128)(2,1)S(1)} %bitcast.95), channel_id=1, source_target_pairs={{0,8},{8,16},{16,24},{24,32},{32,40},{40,48},{48,56},{56,64},{64,7... | collective-permute-start | bytes 1572872 | tf_op jit(solution)/shard_map/ppermute | solution.py:18
  326.0 6.6 %collective-permute-start.1 = (bf16[256,1024]{0,1:T(8,128)(2,1)S(1)}, bf16[256,1024]{0,1:T(8,128)(2,1)}, u32[]{:S(2)}, u32[]{:S(2)}) collective-permute-start(bf16[256,1024]{0,1:T(8,128)(2,1)S(1)} %bitcast.96), channel_id=1, source_target_pairs={{8,0},{16,8},{24,16},{32,24},{40,32},{48,40},{56,48},{64,56},{72,6... | collective-permute-start | bytes 1572872 | tf_op jit(solution)/shard_map/ppermute | solution.py:19
  327.3 6.1 %copy-start.9 = (s32[768]{0:T(1024)S(1)}, s32[768]{0:T(1024)}, u32[]{:S(2)}) copy-start(s32[768]{0:T(1024)} %iota_add_fusion.2) | copy-start | bytes 9220
  327.4 6.1 %copy-start.12 = (s32[256]{0:T(256)S(1)}, s32[256]{0:T(256)}, u32[]{:S(2)}) copy-start(s32[256]{0:T(256)} %param.18) | copy-start | bytes 3076
  327.4 6.1 %copy-start.13 = (s32[256]{0:T(256)S(1)}, s32[256]{0:T(256)}, u32[]{:S(2)}) copy-start(s32[256]{0:T(256)} %get-tuple-element.172) | copy-start | bytes 3076
  327.4 6.1 %copy-start.14 = (f32[256]{0:T(256)S(1)}, f32[256]{0:T(256)}, u32[]{:S(2)}) copy-start(f32[256]{0:T(256)} %get-tuple-element.173) | copy-start | bytes 3076
  333.5 3.4 copy-start.15
  340.2 186.4 %reduce-scatter.2.cloned.1.call-start = ((), (), s32[]{:S(2)}) async-start(), calls=%async_computation.4 | async-start | bytes 7569408 | tf_op jit(solution)/shard_map/reduce_scatter | solution.py:116
  348.0 81.2 %copy-start.8 = (f32[256]{0:T(256)S(1)}, f32[256]{0:T(256)}, u32[]{:S(2)}) copy-start(f32[256]{0:T(256)} %get-tuple-element.170) | copy-start | bytes 3076
  (35 other events, 29.5 us)
Sparse Core Ops, SparseCore 0:
  10.6 51.4 all-gather.6
  64.6 48.1 all-gather.8
  115.3 55.1 all-gather.4
  340.3 86.6 all-reduce.1
  431.0 95.6 reduce-scatter.1
where the time goes:
time: 537 us; the launch traced here: 535 us
  waiting for transfers between devices  249 us (46%)
  matrix products  139 us (26%)
  other arithmetic  64.4 us (12%)
  local copies, waits for them, and re-layouts  38.1 us (7%)
  blocking collectives  24.4 us (5%)
  between operations  14 us (3%)
    reduce_scatter x1, waiting for transfers between devices, body(): lax.psum_scatter(lax.dot_general(normed, residual_grad, (((0,), (0,)), ((...  94.9 us
    psum x1, waiting for transfers between devices, body(): lax.psum(normed_grad.astype(jnp.bfloat16), 'tp').astype(jnp.float32)  79 us
    dot_general x16, matrix products, attend_block(): jnp.einsum('hgqk,khd->hgqd', weights.astype(jnp.bfloat16), values_here, p...  63.5 us
    dot_general x16, matrix products, attend_block(): jnp.einsum('qhgd,khd->hgqk', queries, keys_here, preferred_element_type=j...  60 us
    all_gather x1, waiting for transfers between devices, body(): value_piece = lax.all_gather(teacher_value, 'seq', axis=0, tiled=True)  50.7 us
    all_gather x1, blocking collectives, body(): doc_piece = lax.all_gather(doc_wire, 'seq', axis=0, tiled=True)  24.4 us
    all_gather x1, waiting for transfers between devices, body(): key_piece = lax.all_gather(teacher_key, 'seq', axis=0, tiled=True)  22.5 us
    dynamic_slice x16, local copies, waits for them, and re-layouts, body(): lax.scan(one_block, carry, (key_blocks, value_blocks, doc_blocks, offsets))  21.8 us
  transfers between devices with their start and end apart: 7, of which 4 were waited for; matrix products, arithmetic and copies ran while one was open for 42% of the time, Pallas kernels for 0%

commit v1 on v0

v1 whole, which is shorter than its diff:
```python
import math

import jax
import jax.numpy as jnp
from jax import lax
from jax.experimental import pallas as pl
from jax.experimental.pallas import tpu as pltpu
from jax.sharding import PartitionSpec as P

MESH = pl.DeviceIdType.MESH
F32, BF16 = jnp.float32, jnp.bfloat16
HEAD = 128
T = 256
WIDE = 3584
FEAT = 1024
BIG = float(2**20)
EXP_SCALE = math.log2(math.e) / math.sqrt(HEAD)
REACH = 12
HALO = 80
EVENTS = 176

NT = (((1,), (1,)), ((), ()))


def dot(a, b):
    return jnp.dot(a, b, preferred_element_type=F32)


def dot_nt(a, b):
    return lax.dot_general(a, b, NT, preferred_element_type=F32)


def kernel(
    q_ref, k_ref, v_ref, seg_ref, sh_ref, gain_ref, w_ref, start_ref, count_ref,
    gp_ref, gh_ref,
    kbuf, vbuf, kt_ref, wbuf, qa, m_ref, acc_ref, to_ref,
    normed, nt_ref, nsib, ht_ref, gt_ref, sc_ref, sct_ref, p_ref, r_ref, rsib,
    in_own, in_all, ngb, zrp, zrm,
    ga, gb, ra0p, ra0m, ra1p, ra1m, rb0p, rb0m, rb1p, rb1m,
    ha, hb, sa0p, sa0m, sa1p, sa1m, sb0p, sb0m, sb1p, sb1m,
    send_sems, recv_sems,
):
    i = lax.axis_index("seq")
    z = lax.axis_index("tp")
    c = lax.rem(i, 2)
    t = lax.div(i, 2)
    y = lax.rem(t, 4)
    x = lax.div(t, 4)
    oc = 1 - c

    def mod4(v):
        return lax.rem(v + 8, 4)

    def seq_dev(xx, yy, cc):
        return {"seq": (xx * 4 + yy) * 2 + cc}

    dev_x = {1: seq_dev(mod4(x + 1), y, c), -1: seq_dev(mod4(x - 1), y, c)}
    dev_y = {1: seq_dev(x, mod4(y + 1), c), -1: seq_dev(x, mod4(y - 1), c)}
    dev_z = {d: {"tp": lax.rem(z + d + 8, 8)} for d in (1, -1)}
    sib = seq_dev(x, y, oc)

    barrier = pltpu.get_barrier_semaphore()
    partners = [dev_x[1], dev_x[-1], dev_y[1], dev_y[-1], sib, {"seq": lax.rem(i + 2 * c + 31, 32)}]
    partners += [{"tp": lax.rem(z + d, 8)} for d in range(1, 8)]
    for device in partners:
        pl.semaphore_signal(barrier, inc=1, device_id=device, device_id_type=MESH)

    counter = [0]
    sent = []

    class Send:
        def __init__(self, src, dst, device, arrive=None):
            n = counter[0]
            counter[0] += 1
            self.parts = (n, device)
            self.copy = self.make(src, dst)
            self.copy.start()
            sent.append(self.copy)
            self.arrive = dst if arrive is None else arrive

        def make(self, src, dst):
            n, device = self.parts
            return pltpu.make_async_remote_copy(
                src_ref=src, dst_ref=dst, send_sem=send_sems.at[n], recv_sem=recv_sems.at[n],
                device_id=device, device_id_type=MESH,
            )

        def wait(self):
            self.make(self.arrive, self.arrive).wait_recv()

    def drain():
        for copy in sent:
            copy.wait_send()
        sent.clear()

    class Gather:
        def __init__(self, view, column, x_first):
            self.view, self.column_view, self.x_first = view, column, x_first
            self.dev_a, self.dev_b = (dev_x, dev_y) if x_first else (dev_y, dev_x)
            self.p2, self.f2, self.sibs = {}, {}, []

        def at(self, da, db, part=None):
            dx, dy = (da, db) if self.x_first else (db, da)
            return self.view(mod4(x + dx), mod4(y + dy), part)

        def to_a(self, sign, da, part=None):
            ref = self.at(da, 0, part)
            return Send(ref, ref, self.dev_a[sign], self.at(da - sign, 0, part))

        def to_b(self, sign, da, db, part=None):
            ref = self.at(da, db, part)
            return Send(ref, ref, self.dev_b[sign], self.at(da, db - sign, part))

        def to_sib(self, db):
            b = mod4((y if self.x_first else x) + db)
            ref = self.column_view(b, c)
            self.sibs.append(Send(ref, ref, sib, self.column_view(b, oc)))

        def stage0(self):
            self.p1 = {s: self.to_a(s, 0) for s in (1, -1)}
            for s in (1, -1):
                self.p2[s, 0] = self.to_b(s, 0, 0)

        def stage1(self):
            self.f1 = {}
            for s, part in ((1, 0), (-1, 1)):
                self.p1[s].wait()
                self.f1[s] = self.to_a(s, -s, part)
                for sb in (1, -1):
                    self.p2[sb, -s] = self.to_b(sb, -s, 0)
            self.forward(0)

        def forward(self, da):
            for s, part in ((1, 0), (-1, 1)):
                self.p2[s, da].wait()
                self.f2[s, da] = self.to_b(s, da, -s, part)

        def stage2(self):
            for s in (1, -1):
                self.f1[s].wait()
            for sb in (1, -1):
                self.p2[sb, 2] = self.to_b(sb, 2, 0)
            self.forward(-1)
            self.forward(1)
            self.to_sib(0)

        def stage3(self):
            self.forward(2)
            self.to_sib(-1)
            self.to_sib(1)

        def stage4(self):
            for key in self.f2:
                self.f2[key].wait()
            self.to_sib(2)

        def stage5(self, first=0):
            for s in self.sibs[first:]:
                s.wait()

    def k_view(xx, yy, part):
        return kbuf.at[xx, yy, c] if part is None else kbuf.at[xx, yy, c, pl.ds((0, 128)[part], (128, 144)[part])]

    def v_view(xx, yy, part):
        return vbuf.at[xx, yy, c] if part is None else vbuf.at[xx, yy, c, pl.ds(128 * part, 128)]

    def w_view(first):
        def view(xx, yy, part):
            if part is None:
                return wbuf.at[xx, yy, c, :, pl.ds(first, 512)]
            return wbuf.at[xx, yy, c, :, pl.ds(first + 256 * part, 256)]

        return view

    gather_k = Gather(k_view, lambda b, cc: kbuf.at[:, b, cc], True)
    gather_v = Gather(v_view, lambda b, cc: vbuf.at[b, :, cc], False)
    gather_w0 = Gather(w_view(0), lambda b, cc: wbuf.at[:, b, cc, :, pl.ds(0, 512)], True)
    gather_w1 = Gather(w_view(512), lambda b, cc: wbuf.at[b, :, cc, :, pl.ds(512, 512)], False)

    seg = seg_ref[...]
    below1 = jnp.sum((seg < 1).astype(F32), axis=1, keepdims=True)
    below2 = jnp.sum((seg < 2).astype(F32), axis=1, keepdims=True)
    strip_row = lax.broadcasted_iota(jnp.int32, (16, 128), 0)
    kbuf[x, y, c, 0:T, :] = k_ref[...]
    kbuf[x, y, c, T : T + 16, :] = jnp.where(strip_row < 8, below1, below2).astype(BF16)
    vbuf[x, y, c] = v_ref[...]
    wbuf[x, y, c] = w_ref[...]

    pl.semaphore_wait(barrier, len(partners))

    gather_k.stage0()
    gather_v.stage0()

    squares = jnp.zeros((T, 128), F32)
    for piece in range(WIDE // 128):
        h = sh_ref[:, piece * 128 : (piece + 1) * 128].astype(F32)
        squares = squares + h * h
    mean = jnp.sum(squares, axis=1, keepdims=True) * (1.0 / WIDE)
    scale = lax.rsqrt(mean + 1e-6)
    scale_wide = jnp.broadcast_to(scale, (T, 128))
    sc_ref[...] = scale_wide
    sct_ref[...] = jnp.transpose(scale_wide)[0:8, :]

    def norm_piece(piece, carry):
        cols = pl.ds(pl.multiple_of(piece * 896, 128), 896)
        h = sh_ref[:, cols]
        gain = jnp.concatenate([gain_ref[pl.ds(piece * 7 + n, 1), :] for n in range(7)], axis=1)
        value = (h.astype(F32) * sc_ref[:, 0:1] * gain).astype(BF16)
        normed[:, cols] = value
        nt_ref[piece] = jnp.transpose(value).reshape(4, 2, 112, T)

        @pl.when(piece == lax.div(z, 2))
        def _():
            ht_ref[...] = jnp.transpose(h)
            gt_ref[...] = jnp.transpose(jnp.broadcast_to(gain, (128, 896)))

        return carry

    lax.fori_loop(0, 4, norm_piece, 0)

    send_nt = Send(nt_ref.at[:, :, oc], nsib, sib)
    gather_k.stage1()
    gather_v.stage1()

    rows = lax.broadcasted_iota(jnp.int32, (T, 128), 0).astype(F32)
    lanes = lax.broadcasted_iota(jnp.int32, (T, 128), 1).astype(F32)

    def doc_of(n1, n2):
        return jnp.where(rows >= n1, 1.0, 0.0) + jnp.where(rows >= n2, 1.0, 0.0)

    one_hot = jnp.where(doc_of(below1, below2) == lanes, 1.0, 0.0).astype(BF16)
    for h in range(8):
        qa[h, :, 0:HEAD] = q_ref[:, h * HEAD : (h + 1) * HEAD]
        qa[h, :, HEAD : 2 * HEAD] = one_hot

    doc_id = lax.broadcasted_iota(jnp.int32, (HEAD, T), 0).astype(F32)
    key_id = lax.broadcasted_iota(jnp.int32, (HEAD, T), 1).astype(F32)

    def build_keys(tt):
        xx, yy = lax.div(tt, 4), lax.rem(tt, 4)
        for cc in range(2):
            at = slice(cc * T, (cc + 1) * T)
            strip = kbuf[xx, yy, cc, T : T + 16, :].astype(F32)
            doc = jnp.where(key_id >= strip[0:1, 0:1], 1.0, 0.0) + jnp.where(key_id >= strip[8:9, 0:1], 1.0, 0.0)
            kt_ref[tt, 0:HEAD, at] = jnp.transpose(kbuf[xx, yy, cc, 0:T, :])
            kt_ref[tt, HEAD : 2 * HEAD, at] = jnp.where(doc == doc_id, 0.0, -BIG).astype(BF16)

    ones = jnp.ones((2 * T, HEAD), BF16)

    def wide(v, n):
        return jnp.concatenate([v] * n, axis=1)

    def attend_chip(tt, own):
        xx, yy = lax.div(tt, 4), lax.rem(tt, 4)
        keys = kt_ref[tt]
        values = jnp.concatenate([jnp.concatenate([vbuf[xx, yy, 0], vbuf[xx, yy, 1]], axis=0), ones], axis=1)
        scores = {0: dot(qa[0], keys)}
        for h in range(8):
            if h < 7:
                scores[h + 1] = dot(qa[h + 1], keys)
            s = scores.pop(h)
            if own:
                row = lax.broadcasted_iota(jnp.int32, (T, 2 * T), 0)
                col = lax.broadcasted_iota(jnp.int32, (T, 2 * T), 1)
                s = jnp.where(col <= row + c * T, s, -2.0 * BIG)
                m = jnp.broadcast_to(jnp.max(s, axis=1, keepdims=True), (T, 128))
            else:
                m_old = m_ref[h]
                m = jnp.maximum(m_old, jnp.max(s, axis=1, keepdims=True))
            p = jnp.exp2(((s - wide(m, 4)) * EXP_SCALE).astype(BF16))
            m_ref[h] = m
            update = dot(p, values)
            if own:
                acc_ref[h] = update
            else:
                alpha = jnp.exp2((m_old - m) * EXP_SCALE)
                acc_ref[h] = acc_ref[h] * wide(alpha, 2) + update

    chips = jnp.minimum(t, REACH)

    def attend(quarter):
        def chip(tt, carry):
            attend_chip(tt, False)
            return carry

        low = t - chips + lax.div(chips * quarter, 4)
        high = t - chips + lax.div(chips * (quarter + 1), 4)
        lax.fori_loop(low, high, chip, 0)

    def finish():
        for h in range(8):
            acc = acc_ref[h]
            out = (acc[:, 0:HEAD] / acc[:, HEAD : 2 * HEAD]).astype(BF16)
            to_ref[128 : 128 + T, h * HEAD : (h + 1) * HEAD] = out
        last = Send(
            to_ref.at[pl.ds(128 + T - HALO, HALO)], to_ref.at[pl.ds(128 - HALO, HALO)],
            {"seq": lax.rem(i + 1, 32)},
        )
        first = Send(
            to_ref.at[pl.ds(128, HALO)], to_ref.at[pl.ds(128 + T, HALO)],
            {"seq": lax.rem(i + 31, 32)},
        )
        return [last, first]

    gather_k.stage2()
    gather_v.stage2()
    gather_k.stage3()
    gather_v.stage3()
    gather_w0.stage0()
    gather_w1.stage0()
    gather_k.sibs[0].wait()
    gather_v.sibs[0].wait()
    build_keys(t)
    attend_chip(t, True)

    def column(ref):
        return jnp.transpose(jnp.broadcast_to(ref[...].astype(F32), (128, T)))

    to_ref[0 : 128 - HALO, :] = jnp.zeros((128 - HALO, FEAT), BF16)
    to_ref[128 + T + HALO : 512, :] = jnp.zeros((128 - HALO, FEAT), BF16)
    span_start = column(start_ref)
    span_count = column(count_ref)
    inverse_count = 1.0 / span_count
    first_row = (i * T - 128).astype(F32)
    row_id = lax.broadcasted_iota(jnp.int32, (T, 512), 1).astype(F32) + first_row
    begin, end = wide(span_start, 4), wide(span_start + span_count, 4)
    select = jnp.where((row_id >= begin) & (row_id < end), 1.0, 0.0).astype(BF16)

    gather_k.stage4()
    gather_v.stage4()
    gather_k.stage5(1)
    gather_v.stage5(1)

    def keys_chip(tt, carry):
        build_keys(tt)
        return carry

    lax.fori_loop(t - chips, t, keys_chip, 0)

    attend(0)
    gather_w0.stage1()
    gather_w1.stage1()
    attend(1)
    gather_w0.stage2()
    gather_w1.stage2()
    attend(2)
    gather_w0.stage3()
    gather_w1.stage3()
    attend(3)
    halos = finish()
    gather_w0.stage4()
    gather_w1.stage4()
    gather_w0.stage5()
    gather_w1.stage5()

    def predict(piece, carry):
        cols = pl.ds(pl.multiple_of(piece * 256, 256), 256)
        total = jnp.zeros((T, 256), F32)
        for xx in range(4):
            total = total + dot(normed[:, xx * 896 : (xx + 1) * 896], wbuf[xx, :, :, :, cols].reshape(896, 256))
        p_ref[:, cols] = total
        return carry

    lax.fori_loop(0, 4, predict, 0)
    for s in halos:
        s.wait()

    inner = jnp.zeros((T, 128), F32)
    for piece in range(4):
        cols = slice(piece * 256, (piece + 1) * 256)
        target = dot(select, to_ref[:, cols]) * wide(inverse_count, 2)
        prediction = p_ref[:, cols]
        residual = (prediction - target).astype(BF16)
        r_ref[:, cols] = residual
        product = residual.astype(F32) * prediction
        inner = inner + product[:, 0:128] + product[:, 128:256]
    send_r = Send(r_ref, rsib, sib)
    inner = jnp.broadcast_to(jnp.sum(inner, axis=1, keepdims=True), (T, 128))
    in_own[...] = jnp.transpose(inner)[0:8, :]
    inners = [Send(in_own, in_all.at[d], {"tp": lax.rem(z + d, 8)}) for d in range(1, 8)]

    def normed_grad(d):
        zz = lax.rem(z + d, 8)
        w = wbuf[lax.div(zz, 2), pl.ds(lax.rem(zz, 2) * 2, 2)].reshape(448, FEAT)
        ngb[d] = dot_nt(w, r_ref[...]).astype(BF16)

    lo, hi = pl.ds(0, 224), pl.ds(224, 224)

    def z_send(step, sign, rows_):
        d = (4 - step if sign == 1 else 4 + step)
        box = zrp if sign == 1 else zrm
        return Send(ngb.at[d, rows_], box.at[step, rows_], dev_z[sign])

    def z_add(step, sign, rows_):
        d = (3 - step if sign == 1 else 5 + step)
        box = zrp if sign == 1 else zrm
        ngb[d, rows_] = (ngb[d, rows_].astype(F32) + box[step, rows_].astype(F32)).astype(BF16)

    normed_grad(4)
    z0p, z0m = z_send(0, 1, lo), z_send(0, -1, hi)

    send_nt.wait()
    send_r.wait()

    def grad_a(d):
        yy = mod4(y + d)
        left = nt_ref[:, yy, c].reshape(448, T)
        left_sib = nsib[:, yy].reshape(448, T)
        block = dot(left, r_ref[:, 0:512]) + dot(left_sib, rsib[:, 0:512])
        ga[d] = block.astype(BF16).reshape(4, 112, 512)

    def grad_b(d):
        xx = mod4(x + d)
        left = nt_ref[xx, :, c].reshape(448, T)
        left_sib = nsib[xx].reshape(448, T)
        block = dot(left, r_ref[:, 512:1024]) + dot(left_sib, rsib[:, 512:1024])
        gb[d] = block.astype(BF16).reshape(4, 112, 512)

    two, four = pl.ds(0, 2), pl.ds(2, 2)

    class Scatter:
        def __init__(self, g, r0p, r0m, r1p, r1m, h, s0p, s0m, s1p, s1m, dev_a, dev_b, b):
            self.g, self.r0, self.r1, self.h = g, {1: r0p, -1: r0m}, {1: r1p, -1: r1m}, h
            self.s0, self.s1 = {1: s0p, -1: s0m}, {1: s1p, -1: s1m}
            self.dev_a, self.dev_b, self.b = dev_a, dev_b, b
            self.part = {1: two, -1: four}
            self.cols = {1: pl.ds(0, 256), -1: pl.ds(256, 256)}

        def first(self):
            self.e0 = {s: Send(self.g.at[2, self.part[s]], self.r0[s], self.dev_a[s]) for s in (1, -1)}

        def second(self):
            self.e1 = {}
            for s, d in ((1, 1), (-1, 3)):
                part = self.part[-s]
                self.e1[s] = [Send(self.g.at[d, part], self.r1[s].at[part], self.dev_a[s])]

        def third(self):
            for s, d in ((1, 1), (-1, 3)):
                part = self.part[s]
                self.e0[s].wait()
                self.g[d, part] = (self.g[d, part].astype(F32) + self.r0[s][...].astype(F32)).astype(BF16)
                self.e1[s].append(Send(self.g.at[d, part], self.r1[s].at[part], self.dev_a[s]))

        def fourth(self):
            for s in (1, -1):
                for e in self.e1[s]:
                    e.wait()
            self.h[...] = (
                self.g[0].astype(F32) + self.r1[1][...].astype(F32) + self.r1[-1][...].astype(F32)
            ).astype(BF16)
            far = mod4(self.b + 2)
            self.f0, self.f1 = {}, {}
            for s in (1, -1):
                self.f0[s] = Send(self.h.at[far, :, self.cols[s]], self.s0[s], self.dev_b[s])
            for s in (1, -1):
                cols = self.cols[-s]
                self.f1[s] = [Send(self.h.at[mod4(self.b + s), :, cols], self.s1[s].at[:, cols], self.dev_b[s])]

        def fifth(self):
            for s in (1, -1):
                cols, near = self.cols[s], mod4(self.b + s)
                self.f0[s].wait()
                self.h[near, :, cols] = (
                    self.h[near, :, cols].astype(F32) + self.s0[s][...].astype(F32)
                ).astype(BF16)
                self.f1[s].append(Send(self.h.at[near, :, cols], self.s1[s].at[:, cols], self.dev_b[s]))

        def result(self):
            for s in (1, -1):
                for e in self.f1[s]:
                    e.wait()
            return self.h[self.b].astype(F32) + self.s1[1][...].astype(F32) + self.s1[-1][...].astype(F32)

    scatter_a = Scatter(ga, ra0p, ra0m, ra1p, ra1m, ha, sa0p, sa0m, sa1p, sa1m, dev_y, dev_x, x)
    scatter_b = Scatter(gb, rb0p, rb0m, rb1p, rb1m, hb, sb0p, sb0m, sb1p, sb1m, dev_x, dev_y, y)

    grad_a(2)
    grad_b(2)
    scatter_a.first()
    scatter_b.first()
    grad_a(1)
    grad_a(3)
    scatter_a.second()
    grad_b(1)
    grad_b(3)
    scatter_b.second()
    normed_grad(3)
    z1p = [z_send(1, 1, hi)]
    normed_grad(5)
    z1m = [z_send(1, -1, lo)]
    z0p.wait()
    z_add(0, 1, lo)
    z1p.append(z_send(1, 1, lo))
    z0m.wait()
    z_add(0, -1, hi)
    z1m.append(z_send(1, -1, hi))
    normed_grad(2)
    normed_grad(6)
    scatter_a.third()
    scatter_b.third()

    def z_pass(step, plus, minus):
        out_p, out_m = [], []
        for n in range(2):
            rows_p, rows_m = (hi, lo)[n], (lo, hi)[n]
            plus[n].wait()
            z_add(step, 1, rows_p)
            out_p.append(z_send(step + 1, 1, rows_p))
            minus[n].wait()
            z_add(step, -1, rows_m)
            out_m.append(z_send(step + 1, -1, rows_m))
        return out_p, out_m

    z2p, z2m = z_pass(1, z1p, z1m)
    normed_grad(1)
    normed_grad(7)
    normed_grad(0)
    grad_a(0)
    grad_b(0)
    z3p, z3m = z_pass(2, z2p, z2m)
    scatter_a.fourth()
    scatter_b.fourth()
    scatter_a.fifth()
    scatter_b.fifth()

    total_inner = in_own[0:1, :]
    for d, e in enumerate(inners):
        e.wait()
        total_inner = total_inner + in_all[d + 1, 0:1, :]
    scale_row = sct_ref[0:1, :]
    factor = total_inner * scale_row * scale_row * (1.0 / WIDE)
    for e in z3p + z3m:
        e.wait()
    mine = pl.ds(lax.rem(z, 2) * 448, 448)
    ng = ngb[0].astype(F32) + zrp[3].astype(F32) + zrm[3].astype(F32)
    u = ng * wide(gt_ref[mine, :], 2)
    gh_ref[...] = u * scale_row - ht_ref[mine, :].astype(F32) * factor

    gp_ref[:, 0:512] = scatter_a.result()
    gp_ref[:, 512:1024] = scatter_b.result()
    drain()


def deliver(gp_in, gh_in, gp_out, gh_out, sems):
    copies = [pltpu.make_async_copy(gp_in, gp_out, sems.at[0]), pltpu.make_async_copy(gh_in, gh_out, sems.at[1])]
    for copy in copies:
        copy.start()
    for copy in copies:
        copy.wait()


def vm(shape, dtype=BF16):
    return pltpu.VMEM(shape, dtype)


def body(teacher_query, teacher_key, teacher_value, t_segment, s_hidden, norm_gain, proj_weight, span_start, span_count):
    spec = pl.BlockSpec(memory_space=pltpu.VMEM)
    scratch = [
        vm((4, 4, 2, T + 16, 128)),
        vm((4, 4, 2, T, 128)),
        vm((16, 2 * HEAD, 2 * T)),
        vm((4, 4, 2, 112, FEAT)),
        vm((8, T, 2 * HEAD)),
        vm((8, T, 128), F32),
        vm((8, T, 2 * HEAD), F32),
        vm((512, FEAT)),
        vm((T, WIDE)),
        vm((4, 4, 2, 112, T)),
        vm((4, 4, 112, T)),
        vm((896, T)),
        vm((896, 128), F32),
        vm((T, 128), F32),
        vm((8, T), F32),
        vm((T, FEAT), F32),
        vm((T, FEAT)),
        vm((T, FEAT)),
        vm((8, T), F32),
        vm((8, 8, T), F32),
        vm((8, 448, T)),
        vm((4, 448, T)),
        vm((4, 448, T)),
        vm((4, 4, 112, 512)),
        vm((4, 4, 112, 512)),
    ]
    scratch += [vm((2, 112, 512)), vm((2, 112, 512)), vm((4, 112, 512)), vm((4, 112, 512))] * 2
    scratch += [vm((4, 112, 512))] * 2
    scratch += [vm((112, 256)), vm((112, 256)), vm((112, 512)), vm((112, 512))] * 2
    scratch += [pltpu.SemaphoreType.DMA((EVENTS,)), pltpu.SemaphoreType.DMA((EVENTS,))]
    grad_proj, grad_hidden = pl.pallas_call(
        kernel,
        out_shape=(jax.ShapeDtypeStruct((112, FEAT), F32), jax.ShapeDtypeStruct((448, T), F32)),
        in_specs=[spec] * 9,
        out_specs=(spec, spec),
        scratch_shapes=scratch,
        compiler_params=pltpu.CompilerParams(
            collective_id=0, has_side_effects=True, vmem_limit_bytes=60 * 2**20
        ),
    )(
        teacher_query, teacher_key, teacher_value, t_segment.reshape(1, T), s_hidden,
        norm_gain.reshape(28, 128), proj_weight, span_start.reshape(1, T), span_count.reshape(1, T),
    )
    anywhere = pl.BlockSpec(memory_space=pl.ANY)
    grad_proj, grad_hidden = pl.pallas_call(
        deliver,
        out_shape=(jax.ShapeDtypeStruct((112, FEAT), F32), jax.ShapeDtypeStruct((448, T), F32)),
        in_specs=[anywhere] * 2,
        out_specs=(anywhere, anywhere),
        scratch_shapes=[pltpu.SemaphoreType.DMA((2,))],
        compiler_params=pltpu.CompilerParams(vmem_limit_bytes=60 * 2**20),
    )(grad_proj, grad_hidden)
    return grad_proj, grad_hidden.T


def solution(mesh):
    return jax.shard_map(
        body,
        mesh=mesh,
        in_specs=(
            P("seq", "tp"),
            P("seq", "tp"),
            P("seq", "tp"),
            P("seq"),
            P("seq", None),
            P(),
            P("seq", "tp"),
            P("seq"),
            P("seq"),
        ),
        out_specs=(P("seq", "tp"), P("seq", "tp")),
        check_vma=False,
    )
```

time: 537 us -> 125 us (0.23)
  waiting for transfers between devices: 249 us -> 0 us
  matrix products: 139 us -> 0 us
  Pallas kernels: 0 us -> 123 us
  other arithmetic: 64.4 us -> 0 us
  local copies, waits for them, and re-layouts: 38.1 us -> 0 us
  blocking collectives: 24.4 us -> 0 us
  between operations: 14 us -> 0.8 us
    dot_general x36 -> x0, matrix products: 139 us -> none  [the longest x16 63.5 us: attend_block(): jnp.einsum('hgqk,khd->hgqd', weights.astype(jnp.bfloat16), values_here, p...]
    pallas_call x0 -> x2, Pallas kernels: none -> 123 us  [the longest x1 94.5 us: body(): pl.pallas_call(kernel, out_shape=(jax.ShapeDtypeStruct((112, FEAT), F32),...]
    reduce_scatter x1 -> x0, waiting for transfers between devices: 94.9 us -> none  [body(): lax.psum_scatter(lax.dot_general(normed, residual_grad, (((0,), (0,)), ((...]
    psum x1 -> x0, waiting for transfers between devices: 79 us -> none  [body(): lax.psum(normed_grad.astype(jnp.bfloat16), 'tp').astype(jnp.float32)]
    all_gather x3 -> x0, waiting for transfers between devices: 73.2 us -> none  [the longest x1 50.7 us: body(): value_piece = lax.all_gather(teacher_value, 'seq', axis=0, tiled=True)]
    all_gather x1 -> x0, blocking collectives: 24.4 us -> none  [body(): doc_piece = lax.all_gather(doc_wire, 'seq', axis=0, tiled=True)]
    dynamic_slice x16 -> x0, local copies, waits for them, and re-layouts: 21.8 us -> none  [body(): lax.scan(one_block, carry, (key_blocks, value_blocks, doc_blocks, offsets))]
    reduce_sum x18 -> x0, other arithmetic: 19.1 us -> none  [the longest x16 16.5 us: attend_block(): totals = totals * factor + jnp.sum(weights, axis=-1)]
  transfers between devices with their start and end apart: 7 -> 0, of which waited for: 4 -> 0; matrix products, arithmetic and copies ran while one was open for 42% -> 0% of each run, Pallas kernels for 0% -> 0%
where the time goes in v1:
time: 125 us; the launch traced here: 124 us
  Pallas kernels  123 us (98%)
    pallas_call x1, Pallas kernels, body(): pl.pallas_call(kernel, out_shape=(jax.ShapeDtypeStruct((112, FEAT), F32),...  94.5 us
    pallas_call x1, Pallas kernels, body(): pl.pallas_call(deliver, out_shape=(jax.ShapeDtypeStruct((112, FEAT), F32)...  28.9 us

profile of v1, /device:TPU:32, one launch (start us, length us, event | category | flops | bytes accessed | tf_op | source)
XLA Modules:
  0.0 124.2 jit_solution(13509636141353538500)
XLA Ops:
  0.6 94.5 %shard_map.104 = (f32[112,1024]{1,0:T(8,128)}, f32[448,256]{1,0:T(8,128)}) custom-call(bf16[256,1024]{1,0:T(8,128)(2,1)} %q_ref.1, bf16[256,128]{1,0:T(8,128)(2,1)} %k_ref.1, bf16[256,128]{1,0:T(8,128)(2,1)} %v_ref.1, s32[1,256]{1,0:T(1,128)} %bitcast.6, bf16[256,3584]{1,0:T(8,128)(2,1)} %sh_ref.1, f32[28,128]{1,0:T(8,128)} %bitcast.5, ...), custom_call_target="tpu_custom_call" | custom-call | tf_op jit(solution)/shard_map/pallas_call | solution.py:590
  95.1 28.9 %shard_map.105 = (f32[112,1024]{1,0:T(8,128)}, f32[448,256]{1,0:T(8,128)}) custom-call(f32[112,1024]{1,0:T(8,128)} %get-tuple-element.6.gp_in, f32[448,256]{1,0:T(8,128)} %get-tuple-element.7.gh_in), custom_call_target="tpu_custom_call" | custom-call | tf_op jit(solution)/shard_map/pallas_call | solution.py:604

commit v2 on v1

--- a/solution.py
+++ b/solution.py
@@ -33,7 +33,7 @@
 def kernel(
     q_ref, k_ref, v_ref, seg_ref, sh_ref, gain_ref, w_ref, start_ref, count_ref,
     gp_ref, gh_ref,
-    kbuf, vbuf, kt_ref, wbuf, qa, m_ref, acc_ref, to_ref,
+    kvbuf, kt_ref, wbuf, qa, m_ref, acc_ref, s_ref, pa_ref, pb_ref, to_ref,
     normed, nt_ref, nsib, ht_ref, gt_ref, sc_ref, sct_ref, p_ref, r_ref, rsib,
     in_own, in_all, ngb, zrp, zrm,
     ga, gb, ra0p, ra0m, ra1p, ra1m, rb0p, rb0m, rb1p, rb1m,
@@ -94,14 +94,13 @@
         sent.clear()
 
     class Gather:
-        def __init__(self, view, column, x_first):
-            self.view, self.column_view, self.x_first = view, column, x_first
-            self.dev_a, self.dev_b = (dev_x, dev_y) if x_first else (dev_y, dev_x)
+        def __init__(self, view, column, a, b, sib_b, dev_a, dev_b):
+            self.view, self.column = view, column
+            self.a, self.b, self.sib_b, self.dev_a, self.dev_b = a, b, sib_b, dev_a, dev_b
             self.p2, self.f2, self.sibs = {}, {}, []
 
         def at(self, da, db, part=None):
-            dx, dy = (da, db) if self.x_first else (db, da)
-            return self.view(mod4(x + dx), mod4(y + dy), part)
+            return self.view(mod4(self.a + da), mod4(self.b + db), part)
 
         def to_a(self, sign, da, part=None):
             ref = self.at(da, 0, part)
@@ -112,9 +111,8 @@
             return Send(ref, ref, self.dev_b[sign], self.at(da, db - sign, part))
 
         def to_sib(self, db):
-            b = mod4((y if self.x_first else x) + db)
-            ref = self.column_view(b, c)
-            self.sibs.append(Send(ref, ref, sib, self.column_view(b, oc)))
+            ref = self.column(mod4(self.b + db), c)
+            self.sibs.append(Send(ref, ref, sib, self.column(mod4(self.sib_b + db), oc)))
 
         def stage0(self):
             self.p1 = {s: self.to_a(s, 0) for s in (1, -1)}
@@ -158,38 +156,40 @@
             for s in self.sibs[first:]:
                 s.wait()
 
-    def k_view(xx, yy, part):
-        return kbuf.at[xx, yy, c] if part is None else kbuf.at[xx, yy, c, pl.ds((0, 128)[part], (128, 144)[part])]
-
-    def v_view(xx, yy, part):
-        return vbuf.at[xx, yy, c] if part is None else vbuf.at[xx, yy, c, pl.ds(128 * part, 128)]
-
-    def w_view(first):
-        def view(xx, yy, part):
+    def kv_view(aa, bb, part):
+        if part is None:
+            return kvbuf.at[c, aa, bb]
+        return kvbuf.at[c, aa, bb, pl.ds((0, 128)[part], (128, 144)[part])]
+
+    def w_view(first, x_first):
+        def view(aa, bb, part):
+            xx, yy = (aa, bb) if x_first else (bb, aa)
             if part is None:
                 return wbuf.at[xx, yy, c, :, pl.ds(first, 512)]
             return wbuf.at[xx, yy, c, :, pl.ds(first + 256 * part, 256)]
 
         return view
 
-    gather_k = Gather(k_view, lambda b, cc: kbuf.at[:, b, cc], True)
-    gather_v = Gather(v_view, lambda b, cc: vbuf.at[b, :, cc], False)
-    gather_w0 = Gather(w_view(0), lambda b, cc: wbuf.at[:, b, cc, :, pl.ds(0, 512)], True)
-    gather_w1 = Gather(w_view(512), lambda b, cc: wbuf.at[b, :, cc, :, pl.ds(512, 512)], False)
+    kv_a, kv_b = oc * x + c * y, oc * y + c * x
+    step_a = {d: seq_dev(mod4(x + d * oc), mod4(y + d * c), c) for d in (1, -1)}
+    step_b = {d: seq_dev(mod4(x + d * c), mod4(y + d * oc), c) for d in (1, -1)}
+    gather_kv = Gather(kv_view, lambda bb, cc: kvbuf.at[cc, :, bb], kv_a, kv_b, kv_a, step_a, step_b)
+    gather_w0 = Gather(w_view(0, True), lambda bb, cc: wbuf.at[:, bb, cc, :, pl.ds(0, 512)], x, y, y, dev_x, dev_y)
+    gather_w1 = Gather(w_view(512, False), lambda bb, cc: wbuf.at[bb, :, cc, :, pl.ds(512, 512)], y, x, x, dev_y, dev_x)
 
     seg = seg_ref[...]
     below1 = jnp.sum((seg < 1).astype(F32), axis=1, keepdims=True)
     below2 = jnp.sum((seg < 2).astype(F32), axis=1, keepdims=True)
     strip_row = lax.broadcasted_iota(jnp.int32, (16, 128), 0)
-    kbuf[x, y, c, 0:T, :] = k_ref[...]
-    kbuf[x, y, c, T : T + 16, :] = jnp.where(strip_row < 8, below1, below2).astype(BF16)
-    vbuf[x, y, c] = v_ref[...]
+    kvbuf[c, kv_a, kv_b, 0:T, 0:HEAD] = k_ref[...]
+    kvbuf[c, kv_a, kv_b, 0:T, HEAD : 2 * HEAD] = v_ref[...]
+    strip = jnp.where(strip_row < 8, below1, below2).astype(BF16)
+    kvbuf[c, kv_a, kv_b, T : T + 16, :] = jnp.concatenate([strip, strip], axis=1)
     wbuf[x, y, c] = w_ref[...]
 
     pl.semaphore_wait(barrier, len(partners))
 
-    gather_k.stage0()
-    gather_v.stage0()
+    gather_kv.stage0()
 
     squares = jnp.zeros((T, 128), F32)
     for piece in range(WIDE // 128):
@@ -216,11 +216,12 @@
 
         return carry
 
-    lax.fori_loop(0, 4, norm_piece, 0)
-
+    lax.fori_loop(0, 1, norm_piece, 0)
+    gather_kv.stage1()
+    lax.fori_loop(1, 3, norm_piece, 0)
+    gather_kv.stage2()
+    lax.fori_loop(3, 4, norm_piece, 0)
     send_nt = Send(nt_ref.at[:, :, oc], nsib, sib)
-    gather_k.stage1()
-    gather_v.stage1()
 
     rows = lax.broadcasted_iota(jnp.int32, (T, 128), 0).astype(F32)
     lanes = lax.broadcasted_iota(jnp.int32, (T, 128), 1).astype(F32)
@@ -230,19 +231,23 @@
 
     one_hot = jnp.where(doc_of(below1, below2) == lanes, 1.0, 0.0).astype(BF16)
     for h in range(8):
-        qa[h, :, 0:HEAD] = q_ref[:, h * HEAD : (h + 1) * HEAD]
-        qa[h, :, HEAD : 2 * HEAD] = one_hot
+        at = pl.ds((h % 4) * T, T)
+        qa[h // 4, at, 0:HEAD] = q_ref[:, h * HEAD : (h + 1) * HEAD]
+        qa[h // 4, at, HEAD : 2 * HEAD] = one_hot
 
     doc_id = lax.broadcasted_iota(jnp.int32, (HEAD, T), 0).astype(F32)
     key_id = lax.broadcasted_iota(jnp.int32, (HEAD, T), 1).astype(F32)
 
+    def blocks(tt):
+        xx, yy = lax.div(tt, 4), lax.rem(tt, 4)
+        return kvbuf.at[0, xx, yy], kvbuf.at[1, yy, xx]
+
     def build_keys(tt):
-        xx, yy = lax.div(tt, 4), lax.rem(tt, 4)
-        for cc in range(2):
+        for cc, block in enumerate(blocks(tt)):
             at = slice(cc * T, (cc + 1) * T)
-            strip = kbuf[xx, yy, cc, T : T + 16, :].astype(F32)
+            strip = block[T : T + 16, 0:HEAD].astype(F32)
             doc = jnp.where(key_id >= strip[0:1, 0:1], 1.0, 0.0) + jnp.where(key_id >= strip[8:9, 0:1], 1.0, 0.0)
-            kt_ref[tt, 0:HEAD, at] = jnp.transpose(kbuf[xx, yy, cc, 0:T, :])
+            kt_ref[tt, 0:HEAD, at] = jnp.transpose(block[0:T, 0:HEAD])
             kt_ref[tt, HEAD : 2 * HEAD, at] = jnp.where(doc == doc_id, 0.0, -BIG).astype(BF16)
 
     ones = jnp.ones((2 * T, HEAD), BF16)
@@ -250,37 +255,60 @@
     def wide(v, n):
         return jnp.concatenate([v] * n, axis=1)
 
-    def attend_chip(tt, own):
-        xx, yy = lax.div(tt, 4), lax.rem(tt, 4)
-        keys = kt_ref[tt]
-        values = jnp.concatenate([jnp.concatenate([vbuf[xx, yy, 0], vbuf[xx, yy, 1]], axis=0), ones], axis=1)
-        scores = {0: dot(qa[0], keys)}
-        for h in range(8):
-            if h < 7:
-                scores[h + 1] = dot(qa[h + 1], keys)
-            s = scores.pop(h)
+    def values_of(tt):
+        v = jnp.concatenate([block[0:T, HEAD : 2 * HEAD] for block in blocks(tt)], axis=0)
+        return jnp.concatenate([v, ones], axis=1)
+
+    def soften(group, scores, weights, own):
+        factors = []
+        for piece in range(8):
+            at = slice(piece * 128, (piece + 1) * 128)
+            s = scores[at, :]
             if own:
-                row = lax.broadcasted_iota(jnp.int32, (T, 2 * T), 0)
-                col = lax.broadcasted_iota(jnp.int32, (T, 2 * T), 1)
+                row = lax.broadcasted_iota(jnp.int32, (128, 2 * T), 0) + (piece % 2) * 128
+                col = lax.broadcasted_iota(jnp.int32, (128, 2 * T), 1)
                 s = jnp.where(col <= row + c * T, s, -2.0 * BIG)
-                m = jnp.broadcast_to(jnp.max(s, axis=1, keepdims=True), (T, 128))
+                m = jnp.broadcast_to(jnp.max(s, axis=1, keepdims=True), (128, 128))
             else:
-                m_old = m_ref[h]
+                m_old = m_ref[group, at, :]
                 m = jnp.maximum(m_old, jnp.max(s, axis=1, keepdims=True))
-            p = jnp.exp2(((s - wide(m, 4)) * EXP_SCALE).astype(BF16))
-            m_ref[h] = m
-            update = dot(p, values)
-            if own:
-                acc_ref[h] = update
-            else:
-                alpha = jnp.exp2((m_old - m) * EXP_SCALE)
-                acc_ref[h] = acc_ref[h] * wide(alpha, 2) + update
+                factors.append(jnp.exp2((m_old - m) * EXP_SCALE))
+            weights[at, :] = jnp.exp2(((s - wide(m, 4)) * EXP_SCALE).astype(BF16))
+            m_ref[group, at, :] = m
+        return factors
+
+    def gather_values(group, weights, values, factors):
+        update = dot(weights[...], values)
+        if not factors:
+            acc_ref[group] = update
+            return
+        for piece, factor in enumerate(factors):
+            at = slice(piece * 128, (piece + 1) * 128)
+            acc_ref[group, at, :] = acc_ref[group, at, :] * wide(factor, 2) + update[at, :]
+
+    def own_chip():
+        keys, values = kt_ref[t], values_of(t)
+        s_a = dot(qa[0], keys)
+        s_b = dot(qa[1], keys)
+        soften(0, s_a, pa_ref, True)
+        gather_values(0, pa_ref, values, None)
+        soften(1, s_b, pb_ref, True)
+        gather_values(1, pb_ref, values, None)
+
+    def attend_chip(tt, upper):
+        values = values_of(tt)
+        s_b = dot(qa[1], kt_ref[tt])
+        factors_a = soften(0, s_ref, pa_ref, False)
+        gather_values(0, pa_ref, values, factors_a)
+        s_ref[...] = dot(qa[0], kt_ref[jnp.minimum(tt + 1, upper)])
+        factors_b = soften(1, s_b, pb_ref, False)
+        gather_values(1, pb_ref, values, factors_b)
 
     chips = jnp.minimum(t, REACH)
 
     def attend(quarter):
         def chip(tt, carry):
-            attend_chip(tt, False)
+            attend_chip(tt, jnp.maximum(t - 1, 0))
             return carry
 
         low = t - chips + lax.div(chips * quarter, 4)
@@ -289,7 +317,7 @@
 
     def finish():
         for h in range(8):
-            acc = acc_ref[h]
+            acc = acc_ref[h // 4, pl.ds((h % 4) * T, T), :]
             out = (acc[:, 0:HEAD] / acc[:, HEAD : 2 * HEAD]).astype(BF16)
             to_ref[128 : 128 + T, h * HEAD : (h + 1) * HEAD] = out
         last = Send(
@@ -302,16 +330,13 @@
         )
         return [last, first]
 
-    gather_k.stage2()
-    gather_v.stage2()
-    gather_k.stage3()
-    gather_v.stage3()
+    gather_kv.stage3()
     gather_w0.stage0()
     gather_w1.stage0()
-    gather_k.sibs[0].wait()
-    gather_v.sibs[0].wait()
+    gather_kv.sibs[0].wait()
     build_keys(t)
-    attend_chip(t, True)
+    own_chip()
+    gather_kv.stage4()
 
     def column(ref):
         return jnp.transpose(jnp.broadcast_to(ref[...].astype(F32), (128, T)))
@@ -326,16 +351,17 @@
     begin, end = wide(span_start, 4), wide(span_start + span_count, 4)
     select = jnp.where((row_id >= begin) & (row_id < end), 1.0, 0.0).astype(BF16)
 
-    gather_k.stage4()
-    gather_v.stage4()
-    gather_k.stage5(1)
-    gather_v.stage5(1)
+    gather_kv.stage5(1)
 
     def keys_chip(tt, carry):
         build_keys(tt)
         return carry
 
     lax.fori_loop(t - chips, t, keys_chip, 0)
+
+    @pl.when(chips > 0)
+    def _():
+        s_ref[...] = dot(qa[0], kt_ref[t - chips])
 
     attend(0)
     gather_w0.stage1()
@@ -542,11 +568,15 @@
     drain()
 
 
-def deliver(gp_in, gh_in, gp_out, gh_out, sems):
-    copies = [pltpu.make_async_copy(gp_in, gp_out, sems.at[0]), pltpu.make_async_copy(gh_in, gh_out, sems.at[1])]
-    for copy in copies:
+def deliver(gp_in, gh_in, gp_out, gh_out, gp, gh, sems):
+    into = [pltpu.make_async_copy(gp_in, gp, sems.at[0]), pltpu.make_async_copy(gh_in, gh, sems.at[1])]
+    out = [pltpu.make_async_copy(gp, gp_out, sems.at[2]), pltpu.make_async_copy(gh, gh_out, sems.at[3])]
+    for copy in into:
         copy.start()
-    for copy in copies:
+    for first, second in zip(into, out):
+        first.wait()
+        second.start()
+    for copy in out:
         copy.wait()
 
 
@@ -557,13 +587,15 @@
 def body(teacher_query, teacher_key, teacher_value, t_segment, s_hidden, norm_gain, proj_weight, span_start, span_count):
     spec = pl.BlockSpec(memory_space=pltpu.VMEM)
     scratch = [
-        vm((4, 4, 2, T + 16, 128)),
-        vm((4, 4, 2, T, 128)),
+        vm((2, 4, 4, T + 16, 2 * HEAD)),
         vm((16, 2 * HEAD, 2 * T)),
         vm((4, 4, 2, 112, FEAT)),
-        vm((8, T, 2 * HEAD)),
-        vm((8, T, 128), F32),
-        vm((8, T, 2 * HEAD), F32),
+        vm((2, 4 * T, 2 * HEAD)),
+        vm((2, 4 * T, 128), F32),
+        vm((2, 4 * T, 2 * HEAD), F32),
+        vm((4 * T, 2 * T), F32),
+        vm((4 * T, 2 * T)),
+        vm((4 * T, 2 * T)),
         vm((512, FEAT)),
         vm((T, WIDE)),
         vm((4, 4, 2, 112, T)),
@@ -606,7 +638,7 @@
         out_shape=(jax.ShapeDtypeStruct((112, FEAT), F32), jax.ShapeDtypeStruct((448, T), F32)),
         in_specs=[anywhere] * 2,
         out_specs=(anywhere, anywhere),
-        scratch_shapes=[pltpu.SemaphoreType.DMA((2,))],
+        scratch_shapes=[vm((112, FEAT), F32), vm((448, T), F32), pltpu.SemaphoreType.DMA((4,))],
         compiler_params=pltpu.CompilerParams(vmem_limit_bytes=60 * 2**20),
     )(grad_proj, grad_hidden)
     return grad_proj, grad_hidden.T

time: 125 us -> 98.3 us (0.79)
  Pallas kernels: 123 us -> 96.6 us
    pallas_call x1, Pallas kernels: 28.9 us -> 1.97 us  [body(): pl.pallas_call(deliver, out_shape=(jax.ShapeDtypeStruct((112, FEAT), F32)...]
where the time goes in v2:
time: 98.3 us; the launch traced here: 97.4 us
  Pallas kernels  96.6 us (98%)
    pallas_call x1, Pallas kernels, body(): pl.pallas_call(kernel, out_shape=(jax.ShapeDtypeStruct((112, FEAT), F32),...  94.6 us
    pallas_call x1, Pallas kernels, body(): pl.pallas_call(deliver, out_shape=(jax.ShapeDtypeStruct((112, FEAT), F32)...  1.97 us

profile of v2, /device:TPU:32, one launch (start us, length us, event | category | flops | bytes accessed | tf_op | source)
XLA Modules:
  0.0 97.4 jit_solution(11968746127006644981)
XLA Ops:
  0.6 94.6 %shard_map.104 = (f32[112,1024]{1,0:T(8,128)}, f32[448,256]{1,0:T(8,128)}) custom-call(bf16[256,1024]{1,0:T(8,128)(2,1)} %q_ref.1, bf16[256,128]{1,0:T(8,128)(2,1)} %k_ref.1, bf16[256,128]{1,0:T(8,128)(2,1)} %v_ref.1, s32[1,256]{1,0:T(1,128)} %bitcast.6, bf16[256,3584]{1,0:T(8,128)(2,1)} %sh_ref.1, f32[28,128]{1,0:T(8,128)} %bitcast.5, ...), custom_call_target="tpu_custom_call" | custom-call | tf_op jit(solution)/shard_map/pallas_call | solution.py:622
  95.2 2.0 %shard_map.105 = (f32[112,1024]{1,0:T(8,128)}, f32[448,256]{1,0:T(8,128)}) custom-call(f32[112,1024]{1,0:T(8,128)} %get-tuple-element.6.gp_in, f32[448,256]{1,0:T(8,128)} %get-tuple-element.7.gh_in), custom_call_target="tpu_custom_call" | custom-call | tf_op jit(solution)/shard_map/pallas_call | solution.py:636

commit v3 on v2

--- a/solution.py
+++ b/solution.py
@@ -31,14 +31,14 @@
 
 
 def kernel(
-    q_ref, k_ref, v_ref, seg_ref, sh_ref, gain_ref, w_ref, start_ref, count_ref,
+    q_hbm, k_ref, v_ref, seg_ref, sh_hbm, gain_ref, w_hbm, start_ref, count_ref,
     gp_ref, gh_ref,
-    kvbuf, kt_ref, wbuf, qa, m_ref, acc_ref, s_ref, pa_ref, pb_ref, to_ref,
+    q_ref, sh_ref, kvbuf, wbuf, qa, m_ref, acc_ref, pa_ref, pb_ref, to_ref,
     normed, nt_ref, nsib, ht_ref, gt_ref, sc_ref, sct_ref, p_ref, r_ref, rsib,
     in_own, in_all, ngb, zrp, zrm,
     ga, gb, ra0p, ra0m, ra1p, ra1m, rb0p, rb0m, rb1p, rb1m,
     ha, hb, sa0p, sa0m, sa1p, sa1m, sb0p, sb0m, sb1p, sb1m,
-    send_sems, recv_sems,
+    send_sems, recv_sems, load_sems,
 ):
     i = lax.axis_index("seq")
     z = lax.axis_index("tp")
@@ -64,6 +64,14 @@
     partners += [{"tp": lax.rem(z + d, 8)} for d in range(1, 8)]
     for device in partners:
         pl.semaphore_signal(barrier, inc=1, device_id=device, device_id_type=MESH)
+
+    loads = [
+        pltpu.make_async_copy(sh_hbm, sh_ref, load_sems.at[0]),
+        pltpu.make_async_copy(w_hbm, wbuf.at[x, y, c], load_sems.at[1]),
+        pltpu.make_async_copy(q_hbm, q_ref, load_sems.at[2]),
+    ]
+    for load in loads:
+        load.start()
 
     counter = [0]
     sent = []
@@ -88,10 +96,10 @@
         def wait(self):
             self.make(self.arrive, self.arrive).wait_recv()
 
-    def drain():
-        for copy in sent:
+    def drain(count):
+        for copy in sent[:count]:
             copy.wait_send()
-        sent.clear()
+        del sent[:count]
 
     class Gather:
         def __init__(self, view, column, a, b, sib_b, dev_a, dev_b):
@@ -185,12 +193,12 @@
     kvbuf[c, kv_a, kv_b, 0:T, HEAD : 2 * HEAD] = v_ref[...]
     strip = jnp.where(strip_row < 8, below1, below2).astype(BF16)
     kvbuf[c, kv_a, kv_b, T : T + 16, :] = jnp.concatenate([strip, strip], axis=1)
-    wbuf[x, y, c] = w_ref[...]
 
     pl.semaphore_wait(barrier, len(partners))
 
     gather_kv.stage0()
 
+    loads[0].wait()
     squares = jnp.zeros((T, 128), F32)
     for piece in range(WIDE // 128):
         h = sh_ref[:, piece * 128 : (piece + 1) * 128].astype(F32)
@@ -220,8 +228,12 @@
     gather_kv.stage1()
     lax.fori_loop(1, 3, norm_piece, 0)
     gather_kv.stage2()
+    loads[1].wait()
+    gather_w0.stage0()
+    gather_w1.stage0()
     lax.fori_loop(3, 4, norm_piece, 0)
     send_nt = Send(nt_ref.at[:, :, oc], nsib, sib)
+    loads[2].wait()
 
     rows = lax.broadcasted_iota(jnp.int32, (T, 128), 0).astype(F32)
     lanes = lax.broadcasted_iota(jnp.int32, (T, 128), 1).astype(F32)
@@ -235,20 +247,22 @@
         qa[h // 4, at, 0:HEAD] = q_ref[:, h * HEAD : (h + 1) * HEAD]
         qa[h // 4, at, HEAD : 2 * HEAD] = one_hot
 
-    doc_id = lax.broadcasted_iota(jnp.int32, (HEAD, T), 0).astype(F32)
-    key_id = lax.broadcasted_iota(jnp.int32, (HEAD, T), 1).astype(F32)
+    doc_id = lax.broadcasted_iota(jnp.int32, (16, T), 0).astype(F32)
+    key_id = lax.broadcasted_iota(jnp.int32, (16, T), 1).astype(F32)
 
     def blocks(tt):
         xx, yy = lax.div(tt, 4), lax.rem(tt, 4)
         return kvbuf.at[0, xx, yy], kvbuf.at[1, yy, xx]
 
-    def build_keys(tt):
-        for cc, block in enumerate(blocks(tt)):
-            at = slice(cc * T, (cc + 1) * T)
+    def keys_of(tt):
+        sides = []
+        for block in blocks(tt):
             strip = block[T : T + 16, 0:HEAD].astype(F32)
             doc = jnp.where(key_id >= strip[0:1, 0:1], 1.0, 0.0) + jnp.where(key_id >= strip[8:9, 0:1], 1.0, 0.0)
-            kt_ref[tt, 0:HEAD, at] = jnp.transpose(block[0:T, 0:HEAD])
-            kt_ref[tt, HEAD : 2 * HEAD, at] = jnp.where(doc == doc_id, 0.0, -BIG).astype(BF16)
+            bias = jnp.where(doc == doc_id, 0.0, -BIG).astype(BF16)
+            rest = jnp.zeros((HEAD - 16, T), BF16)
+            sides.append(jnp.concatenate([jnp.transpose(block[0:T, 0:HEAD]), bias, rest], axis=0))
+        return jnp.concatenate(sides, axis=1)
 
     ones = jnp.ones((2 * T, HEAD), BF16)
 
@@ -286,34 +300,34 @@
             at = slice(piece * 128, (piece + 1) * 128)
             acc_ref[group, at, :] = acc_ref[group, at, :] * wide(factor, 2) + update[at, :]
 
-    def own_chip():
-        keys, values = kt_ref[t], values_of(t)
+    def attend_chip(tt, own):
+        keys, values = keys_of(tt), values_of(tt)
         s_a = dot(qa[0], keys)
         s_b = dot(qa[1], keys)
-        soften(0, s_a, pa_ref, True)
-        gather_values(0, pa_ref, values, None)
-        soften(1, s_b, pb_ref, True)
-        gather_values(1, pb_ref, values, None)
-
-    def attend_chip(tt, upper):
-        values = values_of(tt)
-        s_b = dot(qa[1], kt_ref[tt])
-        factors_a = soften(0, s_ref, pa_ref, False)
+        factors_a = soften(0, s_a, pa_ref, own)
         gather_values(0, pa_ref, values, factors_a)
-        s_ref[...] = dot(qa[0], kt_ref[jnp.minimum(tt + 1, upper)])
-        factors_b = soften(1, s_b, pb_ref, False)
+        factors_b = soften(1, s_b, pb_ref, own)
         gather_values(1, pb_ref, values, factors_b)
 
-    chips = jnp.minimum(t, REACH)
-
-    def attend(quarter):
-        def chip(tt, carry):
-            attend_chip(tt, jnp.maximum(t - 1, 0))
+    def near(n):
+        n = n + jnp.where(n >= 4, 1, 0)
+        return lax.div(n, 3) - 1, lax.rem(n, 3) - 1
+
+    def far(n):
+        return jnp.where(n < 4, 2, n - 5), jnp.where(n < 4, n, 2)
+
+    def attend(place, low, high):
+        def step(n, carry):
+            dx, dy = place(n)
+            tt = mod4(x + dx) * 4 + mod4(y + dy)
+
+            @pl.when((tt < t) & (tt >= t - REACH))
+            def _():
+                attend_chip(tt, False)
+
             return carry
 
-        low = t - chips + lax.div(chips * quarter, 4)
-        high = t - chips + lax.div(chips * (quarter + 1), 4)
-        lax.fori_loop(low, high, chip, 0)
+        lax.fori_loop(low, high, step, 0)
 
     def finish():
         for h in range(8):
@@ -330,14 +344,6 @@
         )
         return [last, first]
 
-    gather_kv.stage3()
-    gather_w0.stage0()
-    gather_w1.stage0()
-    gather_kv.sibs[0].wait()
-    build_keys(t)
-    own_chip()
-    gather_kv.stage4()
-
     def column(ref):
         return jnp.transpose(jnp.broadcast_to(ref[...].astype(F32), (128, T)))
 
@@ -351,31 +357,27 @@
     begin, end = wide(span_start, 4), wide(span_start + span_count, 4)
     select = jnp.where((row_id >= begin) & (row_id < end), 1.0, 0.0).astype(BF16)
 
-    gather_kv.stage5(1)
-
-    def keys_chip(tt, carry):
-        build_keys(tt)
-        return carry
-
-    lax.fori_loop(t - chips, t, keys_chip, 0)
-
-    @pl.when(chips > 0)
-    def _():
-        s_ref[...] = dot(qa[0], kt_ref[t - chips])
-
-    attend(0)
+    gather_kv.stage3()
+    gather_kv.sibs[0].wait()
+    attend_chip(t, True)
+    gather_kv.stage4()
+    gather_kv.sibs[1].wait()
+    gather_kv.sibs[2].wait()
     gather_w0.stage1()
     gather_w1.stage1()
-    attend(1)
+    attend(near, 0, 4)
     gather_w0.stage2()
     gather_w1.stage2()
-    attend(2)
+    attend(near, 4, 8)
+    gather_kv.sibs[3].wait()
     gather_w0.stage3()
     gather_w1.stage3()
-    attend(3)
-    halos = finish()
+    attend(far, 0, 4)
     gather_w0.stage4()
     gather_w1.stage4()
+    attend(far, 4, 7)
+    gathered = len(sent)
+    halos = finish()
     gather_w0.stage5()
     gather_w1.stage5()
 
@@ -392,6 +394,7 @@
         s.wait()
 
     inner = jnp.zeros((T, 128), F32)
+    send_r = []
     for piece in range(4):
         cols = slice(piece * 256, (piece + 1) * 256)
         target = dot(select, to_ref[:, cols]) * wide(inverse_count, 2)
@@ -400,7 +403,9 @@
         r_ref[:, cols] = residual
         product = residual.astype(F32) * prediction
         inner = inner + product[:, 0:128] + product[:, 128:256]
-    send_r = Send(r_ref, rsib, sib)
+        if piece % 2 == 1:
+            half = pl.ds((piece - 1) * 256, 512)
+            send_r.append(Send(r_ref.at[:, half], rsib.at[:, half], sib))
     inner = jnp.broadcast_to(jnp.sum(inner, axis=1, keepdims=True), (T, 128))
     in_own[...] = jnp.transpose(inner)[0:8, :]
     inners = [Send(in_own, in_all.at[d], {"tp": lax.rem(z + d, 8)}) for d in range(1, 8)]
@@ -426,7 +431,7 @@
     z0p, z0m = z_send(0, 1, lo), z_send(0, -1, hi)
 
     send_nt.wait()
-    send_r.wait()
+    send_r[0].wait()
 
     def grad_a(d):
         yy = mod4(y + d)
@@ -502,8 +507,9 @@
     scatter_b = Scatter(gb, rb0p, rb0m, rb1p, rb1m, hb, sb0p, sb0m, sb1p, sb1m, dev_x, dev_y, y)
 
     grad_a(2)
+    scatter_a.first()
+    send_r[1].wait()
     grad_b(2)
-    scatter_a.first()
     scatter_b.first()
     grad_a(1)
     grad_a(3)
@@ -523,6 +529,7 @@
     z1m.append(z_send(1, -1, hi))
     normed_grad(2)
     normed_grad(6)
+    drain(gathered)
     scatter_a.third()
     scatter_b.third()
 
@@ -545,6 +552,7 @@
     grad_a(0)
     grad_b(0)
     z3p, z3m = z_pass(2, z2p, z2m)
+    drain(len(sent) - 8)
     scatter_a.fourth()
     scatter_b.fourth()
     scatter_a.fifth()
@@ -565,7 +573,7 @@
 
     gp_ref[:, 0:512] = scatter_a.result()
     gp_ref[:, 512:1024] = scatter_b.result()
-    drain()
+    drain(len(sent))
 
 
 def deliver(gp_in, gh_in, gp_out, gh_out, gp, gh, sems):
@@ -587,13 +595,13 @@
 def body(teacher_query, teacher_key, teacher_value, t_segment, s_hidden, norm_gain, proj_weight, span_start, span_count):
     spec = pl.BlockSpec(memory_space=pltpu.VMEM)
     scratch = [
+        vm((T, FEAT)),
+        vm((T, WIDE)),
         vm((2, 4, 4, T + 16, 2 * HEAD)),
-        vm((16, 2 * HEAD, 2 * T)),
         vm((4, 4, 2, 112, FEAT)),
         vm((2, 4 * T, 2 * HEAD)),
         vm((2, 4 * T, 128), F32),
         vm((2, 4 * T, 2 * HEAD), F32),
-        vm((4 * T, 2 * T), F32),
         vm((4 * T, 2 * T)),
         vm((4 * T, 2 * T)),
         vm((512, FEAT)),
@@ -618,11 +626,12 @@
     scratch += [vm((2, 112, 512)), vm((2, 112, 512)), vm((4, 112, 512)), vm((4, 112, 512))] * 2
     scratch += [vm((4, 112, 512))] * 2
     scratch += [vm((112, 256)), vm((112, 256)), vm((112, 512)), vm((112, 512))] * 2
-    scratch += [pltpu.SemaphoreType.DMA((EVENTS,)), pltpu.SemaphoreType.DMA((EVENTS,))]
+    scratch += [pltpu.SemaphoreType.DMA((EVENTS,)), pltpu.SemaphoreType.DMA((EVENTS,)), pltpu.SemaphoreType.DMA((3,))]
+    anywhere = pl.BlockSpec(memory_space=pl.ANY)
     grad_proj, grad_hidden = pl.pallas_call(
         kernel,
         out_shape=(jax.ShapeDtypeStruct((112, FEAT), F32), jax.ShapeDtypeStruct((448, T), F32)),
-        in_specs=[spec] * 9,
+        in_specs=[anywhere, spec, spec, spec, anywhere, spec, anywhere, spec, spec],
         out_specs=(spec, spec),
         scratch_shapes=scratch,
         compiler_params=pltpu.CompilerParams(
@@ -632,7 +641,6 @@
         teacher_query, teacher_key, teacher_value, t_segment.reshape(1, T), s_hidden,
         norm_gain.reshape(28, 128), proj_weight, span_start.reshape(1, T), span_count.reshape(1, T),
     )
-    anywhere = pl.BlockSpec(memory_space=pl.ANY)
     grad_proj, grad_hidden = pl.pallas_call(
         deliver,
         out_shape=(jax.ShapeDtypeStruct((112, FEAT), F32), jax.ShapeDtypeStruct((448, T), F32)),

time: 98.3 us -> 94.7 us (0.963)
  Pallas kernels: 96.6 us -> 93.7 us
    pallas_call x1, Pallas kernels: 94.6 us -> 91.7 us  [body(): pl.pallas_call(kernel, out_shape=(jax.ShapeDtypeStruct((112, FEAT), F32),...]
where the time goes in v3:
time: 94.7 us; the launch traced here: 94.5 us
  Pallas kernels  93.7 us (99%)
    pallas_call x1, Pallas kernels, body(): pl.pallas_call(kernel, out_shape=(jax.ShapeDtypeStruct((112, FEAT), F32),...  91.7 us
    pallas_call x1, Pallas kernels, body(): pl.pallas_call(deliver, out_shape=(jax.ShapeDtypeStruct((112, FEAT), F32)...  1.97 us

profile of v3, /device:TPU:32, one launch (start us, length us, event | category | flops | bytes accessed | tf_op | source)
XLA Modules:
  0.0 94.5 jit_solution(11892590040246460104)
XLA Ops:
  0.6 91.7 %shard_map.104 = (f32[112,1024]{1,0:T(8,128)}, f32[448,256]{1,0:T(8,128)}) custom-call(bf16[256,1024]{1,0:T(8,128)(2,1)} %q_hbm.1, bf16[256,128]{1,0:T(8,128)(2,1)} %k_ref.1, bf16[256,128]{1,0:T(8,128)(2,1)} %v_ref.1, s32[1,256]{1,0:T(1,128)} %bitcast.6, bf16[256,3584]{1,0:T(8,128)(2,1)} %sh_hbm.1, f32[28,128]{1,0:T(8,128)} %bitcast.5, ...), custom_call_target="tpu_custom_call" | custom-call | tf_op jit(solution)/shard_map/pallas_call | solution.py:631
  92.3 2.0 %shard_map.105 = (f32[112,1024]{1,0:T(8,128)}, f32[448,256]{1,0:T(8,128)}) custom-call(f32[112,1024]{1,0:T(8,128)} %get-tuple-element.6.gp_in, f32[448,256]{1,0:T(8,128)} %get-tuple-element.7.gh_in), custom_call_target="tpu_custom_call" | custom-call | tf_op jit(solution)/shard_map/pallas_call | solution.py:644

commit v4 on v3

--- a/solution.py
+++ b/solution.py
@@ -17,7 +17,7 @@
 EXP_SCALE = math.log2(math.e) / math.sqrt(HEAD)
 REACH = 12
 HALO = 80
-EVENTS = 176
+EVENTS = 224
 
 NT = (((1,), (1,)), ((), ()))
 
@@ -36,8 +36,7 @@
     q_ref, sh_ref, kvbuf, wbuf, qa, m_ref, acc_ref, pa_ref, pb_ref, to_ref,
     normed, nt_ref, nsib, ht_ref, gt_ref, sc_ref, sct_ref, p_ref, r_ref, rsib,
     in_own, in_all, ngb, zrp, zrm,
-    ga, gb, ra0p, ra0m, ra1p, ra1m, rb0p, rb0m, rb1p, rb1m,
-    ha, hb, sa0p, sa0m, sa1p, sa1m, sb0p, sb0m, sb1p, sb1m,
+    g_ref, r0_ref, r1_ref, h_ref, s0_ref, s1_ref,
     send_sems, recv_sems, load_sems,
 ):
     i = lax.axis_index("seq")
@@ -146,22 +145,21 @@
                 self.f1[s].wait()
             for sb in (1, -1):
                 self.p2[sb, 2] = self.to_b(sb, 2, 0)
+
+        def stage2b(self):
             self.forward(-1)
             self.forward(1)
-            self.to_sib(0)
 
         def stage3(self):
             self.forward(2)
-            self.to_sib(-1)
-            self.to_sib(1)
 
         def stage4(self):
             for key in self.f2:
                 self.f2[key].wait()
             self.to_sib(2)
 
-        def stage5(self, first=0):
-            for s in self.sibs[first:]:
+        def stage5(self):
+            for s in self.sibs:
                 s.wait()
 
     def kv_view(aa, bb, part):
@@ -182,6 +180,10 @@
     step_a = {d: seq_dev(mod4(x + d * oc), mod4(y + d * c), c) for d in (1, -1)}
     step_b = {d: seq_dev(mod4(x + d * c), mod4(y + d * oc), c) for d in (1, -1)}
     gather_kv = Gather(kv_view, lambda bb, cc: kvbuf.at[cc, :, bb], kv_a, kv_b, kv_a, step_a, step_b)
+    def share(da, db):
+        ref = gather_kv.at(da, db)
+        return Send(ref, ref, sib, kvbuf.at[oc, mod4(kv_b + da), mod4(kv_a + db)])
+
     gather_w0 = Gather(w_view(0, True), lambda bb, cc: wbuf.at[:, bb, cc, :, pl.ds(0, 512)], x, y, y, dev_x, dev_y)
     gather_w1 = Gather(w_view(512, False), lambda bb, cc: wbuf.at[bb, :, cc, :, pl.ds(512, 512)], y, x, x, dev_y, dev_x)
 
@@ -197,6 +199,7 @@
     pl.semaphore_wait(barrier, len(partners))
 
     gather_kv.stage0()
+    shared = [share(0, 0)]
 
     loads[0].wait()
     squares = jnp.zeros((T, 128), F32)
@@ -226,13 +229,7 @@
 
     lax.fori_loop(0, 1, norm_piece, 0)
     gather_kv.stage1()
-    lax.fori_loop(1, 3, norm_piece, 0)
-    gather_kv.stage2()
-    loads[1].wait()
-    gather_w0.stage0()
-    gather_w1.stage0()
-    lax.fori_loop(3, 4, norm_piece, 0)
-    send_nt = Send(nt_ref.at[:, :, oc], nsib, sib)
+    near_shared = [share(1, 0), share(-1, 0), share(0, 1), share(0, -1)]
     loads[2].wait()
 
     rows = lax.broadcasted_iota(jnp.int32, (T, 128), 0).astype(F32)
@@ -357,25 +354,45 @@
     begin, end = wide(span_start, 4), wide(span_start + span_count, 4)
     select = jnp.where((row_id >= begin) & (row_id < end), 1.0, 0.0).astype(BF16)
 
+    gather_kv.stage2()
+    far_shared = [share(2, 0)]
+    loads[1].wait()
+    gather_w0.stage0()
+    gather_w1.stage0()
+    shared[0].wait()
+    attend_chip(t, True)
+    gather_kv.stage2b()
+    near_shared += [share(da, db) for da in (1, -1) for db in (1, -1)]
+    lax.fori_loop(1, 4, norm_piece, 0)
+    send_nt = Send(nt_ref.at[:, :, oc], nsib, sib)
     gather_kv.stage3()
-    gather_kv.sibs[0].wait()
-    attend_chip(t, True)
-    gather_kv.stage4()
-    gather_kv.sibs[1].wait()
-    gather_kv.sibs[2].wait()
+    far_shared += [share(2, 1), share(2, -1)]
+    for s in near_shared:
+        s.wait()
+    attend(near, 0, 3)
     gather_w0.stage1()
     gather_w1.stage1()
-    attend(near, 0, 4)
+    attend(near, 3, 6)
+    gather_kv.stage4()
     gather_w0.stage2()
     gather_w1.stage2()
-    attend(near, 4, 8)
-    gather_kv.sibs[3].wait()
-    gather_w0.stage3()
-    gather_w1.stage3()
-    attend(far, 0, 4)
+    gather_w0.to_sib(0)
+    gather_w1.to_sib(0)
+    attend(near, 6, 8)
+    for s in far_shared:
+        s.wait()
+    gather_kv.stage5()
+    gather_w0.stage2b()
+    gather_w1.stage2b()
+    attend(far, 0, 3)
+    for gather in (gather_w0, gather_w1):
+        gather.stage3()
+        gather.to_sib(-1)
+        gather.to_sib(1)
+    attend(far, 3, 5)
     gather_w0.stage4()
     gather_w1.stage4()
-    attend(far, 4, 7)
+    attend(far, 5, 7)
     gathered = len(sent)
     halos = finish()
     gather_w0.stage5()
@@ -438,24 +455,31 @@
         left = nt_ref[:, yy, c].reshape(448, T)
         left_sib = nsib[:, yy].reshape(448, T)
         block = dot(left, r_ref[:, 0:512]) + dot(left_sib, rsib[:, 0:512])
-        ga[d] = block.astype(BF16).reshape(4, 112, 512)
+        block = block.astype(BF16)
+        g_ref[0, d] = block[:, 0:256].reshape(4, 112, 256)
+        g_ref[1, d] = block[:, 256:512].reshape(4, 112, 256)
 
     def grad_b(d):
         xx = mod4(x + d)
         left = nt_ref[xx, :, c].reshape(448, T)
         left_sib = nsib[xx].reshape(448, T)
         block = dot(left, r_ref[:, 512:1024]) + dot(left_sib, rsib[:, 512:1024])
-        gb[d] = block.astype(BF16).reshape(4, 112, 512)
+        block = block.astype(BF16)
+        g_ref[2, d] = block[:, 0:256].reshape(4, 112, 256)
+        g_ref[3, d] = block[:, 256:512].reshape(4, 112, 256)
 
     two, four = pl.ds(0, 2), pl.ds(2, 2)
 
     class Scatter:
-        def __init__(self, g, r0p, r0m, r1p, r1m, h, s0p, s0m, s1p, s1m, dev_a, dev_b, b):
-            self.g, self.r0, self.r1, self.h = g, {1: r0p, -1: r0m}, {1: r1p, -1: r1m}, h
-            self.s0, self.s1 = {1: s0p, -1: s0m}, {1: s1p, -1: s1m}
+        def __init__(self, n, dev_a, dev_b, b):
+            self.g, self.h = g_ref.at[n], h_ref.at[n]
+            self.r0 = {1: r0_ref.at[n, 0], -1: r0_ref.at[n, 1]}
+            self.r1 = {1: r1_ref.at[n, 0], -1: r1_ref.at[n, 1]}
+            self.s0 = {1: s0_ref.at[n, 0], -1: s0_ref.at[n, 1]}
+            self.s1 = {1: s1_ref.at[n, 0], -1: s1_ref.at[n, 1]}
             self.dev_a, self.dev_b, self.b = dev_a, dev_b, b
             self.part = {1: two, -1: four}
-            self.cols = {1: pl.ds(0, 256), -1: pl.ds(256, 256)}
+            self.cols = {1: pl.ds(0, 128), -1: pl.ds(128, 128)}
 
         def first(self):
             self.e0 = {s: Send(self.g.at[2, self.part[s]], self.r0[s], self.dev_a[s]) for s in (1, -1)}
@@ -503,20 +527,22 @@
                     e.wait()
             return self.h[self.b].astype(F32) + self.s1[1][...].astype(F32) + self.s1[-1][...].astype(F32)
 
-    scatter_a = Scatter(ga, ra0p, ra0m, ra1p, ra1m, ha, sa0p, sa0m, sa1p, sa1m, dev_y, dev_x, x)
-    scatter_b = Scatter(gb, rb0p, rb0m, rb1p, rb1m, hb, sb0p, sb0m, sb1p, sb1m, dev_x, dev_y, y)
+    a0, a1 = Scatter(0, dev_y, dev_x, x), Scatter(1, dev_y, dev_x, x)
+    b0, b1 = Scatter(2, dev_x, dev_y, y), Scatter(3, dev_x, dev_y, y)
 
     grad_a(2)
-    scatter_a.first()
+    a0.first()
     send_r[1].wait()
     grad_b(2)
-    scatter_b.first()
+    b0.first()
+    a1.first()
+    b1.first()
     grad_a(1)
     grad_a(3)
-    scatter_a.second()
+    a0.second()
     grad_b(1)
     grad_b(3)
-    scatter_b.second()
+    b0.second()
     normed_grad(3)
     z1p = [z_send(1, 1, hi)]
     normed_grad(5)
@@ -527,11 +553,15 @@
     z0m.wait()
     z_add(0, -1, hi)
     z1m.append(z_send(1, -1, hi))
+    a0.third()
+    b0.third()
+    a1.second()
+    b1.second()
     normed_grad(2)
     normed_grad(6)
+    a1.third()
+    b1.third()
     drain(gathered)
-    scatter_a.third()
-    scatter_b.third()
 
     def z_pass(step, plus, minus):
         out_p, out_m = [], []
@@ -552,11 +582,15 @@
     grad_a(0)
     grad_b(0)
     z3p, z3m = z_pass(2, z2p, z2m)
-    drain(len(sent) - 8)
-    scatter_a.fourth()
-    scatter_b.fourth()
-    scatter_a.fifth()
-    scatter_b.fifth()
+    a0.fourth()
+    b0.fourth()
+    a0.fifth()
+    b0.fifth()
+    a1.fourth()
+    b1.fourth()
+    a1.fifth()
+    b1.fifth()
+    drain(len(sent) - 32)
 
     total_inner = in_own[0:1, :]
     for d, e in enumerate(inners):
@@ -571,9 +605,10 @@
     u = ng * wide(gt_ref[mine, :], 2)
     gh_ref[...] = u * scale_row - ht_ref[mine, :].astype(F32) * factor
 
-    gp_ref[:, 0:512] = scatter_a.result()
-    gp_ref[:, 512:1024] = scatter_b.result()
+    for n, part in enumerate((a0, a1, b0, b1)):
+        gp_ref[:, n * 256 : (n + 1) * 256] = part.result()
     drain(len(sent))
+    assert counter[0] <= EVENTS
 
 
 def deliver(gp_in, gh_in, gp_out, gh_out, gp, gh, sems):
@@ -620,12 +655,13 @@
         vm((8, 448, T)),
         vm((4, 448, T)),
         vm((4, 448, T)),
-        vm((4, 4, 112, 512)),
-        vm((4, 4, 112, 512)),
+        vm((4, 4, 4, 112, 256)),
+        vm((4, 2, 2, 112, 256)),
+        vm((4, 2, 4, 112, 256)),
+        vm((4, 4, 112, 256)),
+        vm((4, 2, 112, 128)),
+        vm((4, 2, 112, 256)),
     ]
-    scratch += [vm((2, 112, 512)), vm((2, 112, 512)), vm((4, 112, 512)), vm((4, 112, 512))] * 2
-    scratch += [vm((4, 112, 512))] * 2
-    scratch += [vm((112, 256)), vm((112, 256)), vm((112, 512)), vm((112, 512))] * 2
     scratch += [pltpu.SemaphoreType.DMA((EVENTS,)), pltpu.SemaphoreType.DMA((EVENTS,)), pltpu.SemaphoreType.DMA((3,))]
     anywhere = pl.BlockSpec(memory_space=pl.ANY)
     grad_proj, grad_hidden = pl.pallas_call(

time: 94.7 us -> 95.4 us (level)
  no operation moved by 1% of the time
where the time goes in v4:
time: 95.4 us; the launch traced here: 95 us
  Pallas kernels  94.1 us (99%)
    pallas_call x1, Pallas kernels, body(): pl.pallas_call(kernel, out_shape=(jax.ShapeDtypeStruct((112, FEAT), F32),...  92.2 us
    pallas_call x1, Pallas kernels, body(): pl.pallas_call(deliver, out_shape=(jax.ShapeDtypeStruct((112, FEAT), F32)...  1.97 us

profile of v4, /device:TPU:32, one launch (start us, length us, event | category | flops | bytes accessed | tf_op | source)
XLA Modules:
  0.0 95.0 jit_solution(2323578824213148726)
XLA Ops:
  0.6 92.2 %shard_map.104 = (f32[112,1024]{1,0:T(8,128)}, f32[448,256]{1,0:T(8,128)}) custom-call(bf16[256,1024]{1,0:T(8,128)(2,1)} %q_hbm.1, bf16[256,128]{1,0:T(8,128)(2,1)} %k_ref.1, bf16[256,128]{1,0:T(8,128)(2,1)} %v_ref.1, s32[1,256]{1,0:T(1,128)} %bitcast.6, bf16[256,3584]{1,0:T(8,128)(2,1)} %sh_hbm.1, f32[28,128]{1,0:T(8,128)} %bitcast.5, ...), custom_call_target="tpu_custom_call" | custom-call | tf_op jit(solution)/shard_map/pallas_call | solution.py:667
  92.8 2.0 %shard_map.105 = (f32[112,1024]{1,0:T(8,128)}, f32[448,256]{1,0:T(8,128)}) custom-call(f32[112,1024]{1,0:T(8,128)} %get-tuple-element.6.gp_in, f32[448,256]{1,0:T(8,128)} %get-tuple-element.7.gh_in), custom_call_target="tpu_custom_call" | custom-call | tf_op jit(solution)/shard_map/pallas_call | solution.py:680

commit v5 on v4

--- a/solution.py
+++ b/solution.py
@@ -230,22 +230,22 @@
     lax.fori_loop(0, 1, norm_piece, 0)
     gather_kv.stage1()
     near_shared = [share(1, 0), share(-1, 0), share(0, 1), share(0, -1)]
+    loads[1].wait()
+    gather_w0.stage0()
+    gather_w1.stage0()
     loads[2].wait()
 
-    rows = lax.broadcasted_iota(jnp.int32, (T, 128), 0).astype(F32)
-    lanes = lax.broadcasted_iota(jnp.int32, (T, 128), 1).astype(F32)
-
-    def doc_of(n1, n2):
-        return jnp.where(rows >= n1, 1.0, 0.0) + jnp.where(rows >= n2, 1.0, 0.0)
-
-    one_hot = jnp.where(doc_of(below1, below2) == lanes, 1.0, 0.0).astype(BF16)
+    doc_row = lax.broadcasted_iota(jnp.int32, (HEAD, T), 0).astype(F32)
+    token = lax.broadcasted_iota(jnp.int32, (HEAD, T), 1).astype(F32)
+    own_doc = jnp.where(token >= below1, 1.0, 0.0) + jnp.where(token >= below2, 1.0, 0.0)
+    one_hot = jnp.where(own_doc == doc_row, 1.0, 0.0).astype(BF16)
     for h in range(8):
         at = pl.ds((h % 4) * T, T)
-        qa[h // 4, at, 0:HEAD] = q_ref[:, h * HEAD : (h + 1) * HEAD]
-        qa[h // 4, at, HEAD : 2 * HEAD] = one_hot
-
-    doc_id = lax.broadcasted_iota(jnp.int32, (16, T), 0).astype(F32)
-    key_id = lax.broadcasted_iota(jnp.int32, (16, T), 1).astype(F32)
+        qa[h // 4, 0:HEAD, at] = jnp.transpose(q_ref[:, h * HEAD : (h + 1) * HEAD])
+        qa[h // 4, HEAD : 2 * HEAD, at] = one_hot
+
+    key_row = lax.broadcasted_iota(jnp.int32, (T, HEAD), 0).astype(F32)
+    doc_lane = lax.broadcasted_iota(jnp.int32, (T, HEAD), 1).astype(F32)
 
     def blocks(tt):
         xx, yy = lax.div(tt, 4), lax.rem(tt, 4)
@@ -255,52 +255,51 @@
         sides = []
         for block in blocks(tt):
             strip = block[T : T + 16, 0:HEAD].astype(F32)
-            doc = jnp.where(key_id >= strip[0:1, 0:1], 1.0, 0.0) + jnp.where(key_id >= strip[8:9, 0:1], 1.0, 0.0)
-            bias = jnp.where(doc == doc_id, 0.0, -BIG).astype(BF16)
-            rest = jnp.zeros((HEAD - 16, T), BF16)
-            sides.append(jnp.concatenate([jnp.transpose(block[0:T, 0:HEAD]), bias, rest], axis=0))
-        return jnp.concatenate(sides, axis=1)
-
-    ones = jnp.ones((2 * T, HEAD), BF16)
+            doc = jnp.where(key_row >= strip[0:1, :], 1.0, 0.0) + jnp.where(key_row >= strip[8:9, :], 1.0, 0.0)
+            bias = jnp.where(doc == doc_lane, 0.0, -BIG).astype(BF16)
+            sides.append(jnp.concatenate([block[0:T, 0:HEAD], bias], axis=1))
+        return jnp.concatenate(sides, axis=0)
+
+    ones = jnp.ones((16, 2 * T), BF16)
 
     def wide(v, n):
         return jnp.concatenate([v] * n, axis=1)
 
     def values_of(tt):
-        v = jnp.concatenate([block[0:T, HEAD : 2 * HEAD] for block in blocks(tt)], axis=0)
-        return jnp.concatenate([v, ones], axis=1)
+        v = jnp.concatenate([jnp.transpose(block[0:T, HEAD : 2 * HEAD]) for block in blocks(tt)], axis=1)
+        return jnp.concatenate([v, ones], axis=0)
 
     def soften(group, scores, weights, own):
         factors = []
         for piece in range(8):
             at = slice(piece * 128, (piece + 1) * 128)
-            s = scores[at, :]
+            s = scores[:, at]
             if own:
-                row = lax.broadcasted_iota(jnp.int32, (128, 2 * T), 0) + (piece % 2) * 128
-                col = lax.broadcasted_iota(jnp.int32, (128, 2 * T), 1)
-                s = jnp.where(col <= row + c * T, s, -2.0 * BIG)
-                m = jnp.broadcast_to(jnp.max(s, axis=1, keepdims=True), (128, 128))
+                row = lax.broadcasted_iota(jnp.int32, (2 * T, 128), 0)
+                col = lax.broadcasted_iota(jnp.int32, (2 * T, 128), 1) + (piece % 2) * 128
+                s = jnp.where(row <= col + c * T, s, -2.0 * BIG)
+                m = jnp.max(s, axis=0, keepdims=True)
             else:
-                m_old = m_ref[group, at, :]
-                m = jnp.maximum(m_old, jnp.max(s, axis=1, keepdims=True))
+                m_old = m_ref[group, 0:1, at]
+                m = jnp.maximum(m_old, jnp.max(s, axis=0, keepdims=True))
                 factors.append(jnp.exp2((m_old - m) * EXP_SCALE))
-            weights[at, :] = jnp.exp2(((s - wide(m, 4)) * EXP_SCALE).astype(BF16))
-            m_ref[group, at, :] = m
+            weights[:, at] = jnp.exp2(((s - m) * EXP_SCALE).astype(BF16))
+            m_ref[group, 0:1, at] = m
         return factors
 
     def gather_values(group, weights, values, factors):
-        update = dot(weights[...], values)
+        update = dot(values, weights[...])
         if not factors:
             acc_ref[group] = update
             return
         for piece, factor in enumerate(factors):
             at = slice(piece * 128, (piece + 1) * 128)
-            acc_ref[group, at, :] = acc_ref[group, at, :] * wide(factor, 2) + update[at, :]
+            acc_ref[group, :, at] = acc_ref[group, :, at] * factor + update[:, at]
 
     def attend_chip(tt, own):
         keys, values = keys_of(tt), values_of(tt)
-        s_a = dot(qa[0], keys)
-        s_b = dot(qa[1], keys)
+        s_a = dot(keys, qa[0])
+        s_b = dot(keys, qa[1])
         factors_a = soften(0, s_a, pa_ref, own)
         gather_values(0, pa_ref, values, factors_a)
         factors_b = soften(1, s_b, pb_ref, own)
@@ -328,9 +327,9 @@
 
     def finish():
         for h in range(8):
-            acc = acc_ref[h // 4, pl.ds((h % 4) * T, T), :]
-            out = (acc[:, 0:HEAD] / acc[:, HEAD : 2 * HEAD]).astype(BF16)
-            to_ref[128 : 128 + T, h * HEAD : (h + 1) * HEAD] = out
+            at = pl.ds((h % 4) * T, T)
+            out = acc_ref[h // 4, 0:HEAD, at] / acc_ref[h // 4, HEAD : HEAD + 1, at]
+            to_ref[128 : 128 + T, h * HEAD : (h + 1) * HEAD] = jnp.transpose(out.astype(BF16))
         last = Send(
             to_ref.at[pl.ds(128 + T - HALO, HALO)], to_ref.at[pl.ds(128 - HALO, HALO)],
             {"seq": lax.rem(i + 1, 32)},
@@ -356,43 +355,39 @@
 
     gather_kv.stage2()
     far_shared = [share(2, 0)]
-    loads[1].wait()
-    gather_w0.stage0()
-    gather_w1.stage0()
     shared[0].wait()
     attend_chip(t, True)
     gather_kv.stage2b()
     near_shared += [share(da, db) for da in (1, -1) for db in (1, -1)]
     lax.fori_loop(1, 4, norm_piece, 0)
     send_nt = Send(nt_ref.at[:, :, oc], nsib, sib)
+    for s in near_shared:
+        s.wait()
+    gather_w0.stage1()
+    gather_w1.stage1()
+    attend(near, 0, 2)
     gather_kv.stage3()
     far_shared += [share(2, 1), share(2, -1)]
-    for s in near_shared:
-        s.wait()
-    attend(near, 0, 3)
-    gather_w0.stage1()
-    gather_w1.stage1()
-    attend(near, 3, 6)
+    attend(near, 2, 4)
+    for gather in (gather_w0, gather_w1):
+        gather.stage2()
+        gather.to_sib(0)
+    attend(near, 4, 6)
     gather_kv.stage4()
-    gather_w0.stage2()
-    gather_w1.stage2()
-    gather_w0.to_sib(0)
-    gather_w1.to_sib(0)
+    gather_w0.stage2b()
+    gather_w1.stage2b()
     attend(near, 6, 8)
     for s in far_shared:
         s.wait()
     gather_kv.stage5()
-    gather_w0.stage2b()
-    gather_w1.stage2b()
-    attend(far, 0, 3)
     for gather in (gather_w0, gather_w1):
         gather.stage3()
         gather.to_sib(-1)
         gather.to_sib(1)
-    attend(far, 3, 5)
+    attend(far, 0, 3)
     gather_w0.stage4()
     gather_w1.stage4()
-    attend(far, 5, 7)
+    attend(far, 3, 7)
     gathered = len(sent)
     halos = finish()
     gather_w0.stage5()
@@ -530,6 +525,15 @@
     a0, a1 = Scatter(0, dev_y, dev_x, x), Scatter(1, dev_y, dev_x, x)
     b0, b1 = Scatter(2, dev_x, dev_y, y), Scatter(3, dev_x, dev_y, y)
 
+    def z_half(step, n, plus, minus):
+        rows_p, rows_m = (hi, lo)[n], (lo, hi)[n]
+        plus[n].wait()
+        z_add(step, 1, rows_p)
+        out_p = z_send(step + 1, 1, rows_p)
+        minus[n].wait()
+        z_add(step, -1, rows_m)
+        return out_p, z_send(step + 1, -1, rows_m)
+
     grad_a(2)
     a0.first()
     send_r[1].wait()
@@ -537,53 +541,43 @@
     b0.first()
     a1.first()
     b1.first()
-    grad_a(1)
-    grad_a(3)
-    a0.second()
-    grad_b(1)
-    grad_b(3)
-    b0.second()
     normed_grad(3)
     z1p = [z_send(1, 1, hi)]
     normed_grad(5)
     z1m = [z_send(1, -1, lo)]
+    grad_a(1)
+    grad_a(3)
+    a0.second()
     z0p.wait()
     z_add(0, 1, lo)
     z1p.append(z_send(1, 1, lo))
     z0m.wait()
     z_add(0, -1, hi)
     z1m.append(z_send(1, -1, hi))
+    grad_b(1)
+    grad_b(3)
+    b0.second()
+    normed_grad(2)
+    normed_grad(6)
     a0.third()
     b0.third()
     a1.second()
     b1.second()
-    normed_grad(2)
-    normed_grad(6)
+    z2 = [z_half(1, 0, z1p, z1m)]
     a1.third()
     b1.third()
-    drain(gathered)
-
-    def z_pass(step, plus, minus):
-        out_p, out_m = [], []
-        for n in range(2):
-            rows_p, rows_m = (hi, lo)[n], (lo, hi)[n]
-            plus[n].wait()
-            z_add(step, 1, rows_p)
-            out_p.append(z_send(step + 1, 1, rows_p))
-            minus[n].wait()
-            z_add(step, -1, rows_m)
-            out_m.append(z_send(step + 1, -1, rows_m))
-        return out_p, out_m
-
-    z2p, z2m = z_pass(1, z1p, z1m)
+    z2.append(z_half(1, 1, z1p, z1m))
+    z2p, z2m = zip(*z2)
     normed_grad(1)
     normed_grad(7)
-    normed_grad(0)
     grad_a(0)
     grad_b(0)
-    z3p, z3m = z_pass(2, z2p, z2m)
+    normed_grad(0)
+    drain(gathered)
+    z3 = [z_half(2, 0, z2p, z2m)]
     a0.fourth()
     b0.fourth()
+    z3.append(z_half(2, 1, z2p, z2m))
     a0.fifth()
     b0.fifth()
     a1.fourth()
@@ -598,8 +592,9 @@
         total_inner = total_inner + in_all[d + 1, 0:1, :]
     scale_row = sct_ref[0:1, :]
     factor = total_inner * scale_row * scale_row * (1.0 / WIDE)
-    for e in z3p + z3m:
-        e.wait()
+    for pair in z3:
+        for e in pair:
+            e.wait()
     mine = pl.ds(lax.rem(z, 2) * 448, 448)
     ng = ngb[0].astype(F32) + zrp[3].astype(F32) + zrm[3].astype(F32)
     u = ng * wide(gt_ref[mine, :], 2)
@@ -634,11 +629,11 @@
         vm((T, WIDE)),
         vm((2, 4, 4, T + 16, 2 * HEAD)),
         vm((4, 4, 2, 112, FEAT)),
-        vm((2, 4 * T, 2 * HEAD)),
-        vm((2, 4 * T, 128), F32),
-        vm((2, 4 * T, 2 * HEAD), F32),
-        vm((4 * T, 2 * T)),
-        vm((4 * T, 2 * T)),
+        vm((2, 2 * HEAD, 4 * T)),
+        vm((2, 8, 4 * T), F32),
+        vm((2, HEAD + 16, 4 * T), F32),
+        vm((2 * T, 4 * T)),
+        vm((2 * T, 4 * T)),
         vm((512, FEAT)),
         vm((T, WIDE)),
         vm((4, 4, 2, 112, T)),

time: 95.4 us -> 96.5 us (1.012)
  Pallas kernels: 94.1 us -> 95.5 us
    pallas_call x1, Pallas kernels: 92.2 us -> 93.5 us  [body(): pl.pallas_call(kernel, out_shape=(jax.ShapeDtypeStruct((112, FEAT), F32),...]
where the time goes in v5:
time: 96.5 us; the launch traced here: 96.3 us
  Pallas kernels  95.5 us (99%)
    pallas_call x1, Pallas kernels, body(): pl.pallas_call(kernel, out_shape=(jax.ShapeDtypeStruct((112, FEAT), F32),...  93.5 us
    pallas_call x1, Pallas kernels, body(): pl.pallas_call(deliver, out_shape=(jax.ShapeDtypeStruct((112, FEAT), F32)...  1.97 us

profile of v5, /device:TPU:32, one launch (start us, length us, event | category | flops | bytes accessed | tf_op | source)
XLA Modules:
  0.0 96.3 jit_solution(7209928692942462147)
XLA Ops:
  0.6 93.5 %shard_map.104 = (f32[112,1024]{1,0:T(8,128)}, f32[448,256]{1,0:T(8,128)}) custom-call(bf16[256,1024]{1,0:T(8,128)(2,1)} %q_hbm.1, bf16[256,128]{1,0:T(8,128)(2,1)} %k_ref.1, bf16[256,128]{1,0:T(8,128)(2,1)} %v_ref.1, s32[1,256]{1,0:T(1,128)} %bitcast.6, bf16[256,3584]{1,0:T(8,128)(2,1)} %sh_hbm.1, f32[28,128]{1,0:T(8,128)} %bitcast.5, ...), custom_call_target="tpu_custom_call" | custom-call | tf_op jit(solution)/shard_map/pallas_call | solution.py:662
  94.1 2.0 %shard_map.105 = (f32[112,1024]{1,0:T(8,128)}, f32[448,256]{1,0:T(8,128)}) custom-call(f32[112,1024]{1,0:T(8,128)} %get-tuple-element.6.gp_in, f32[448,256]{1,0:T(8,128)} %get-tuple-element.7.gh_in), custom_call_target="tpu_custom_call" | custom-call | tf_op jit(solution)/shard_map/pallas_call | solution.py:675

commit v6 on v5

--- a/solution.py
+++ b/solution.py
@@ -158,6 +158,14 @@
                 self.f2[key].wait()
             self.to_sib(2)
 
+        def stage4_by_shard(self):
+            for da in (0, -1, 1, 2):
+                for sign in (1, -1):
+                    self.f2[sign, da].wait()
+                at = mod4(self.a + da), mod4(self.b + 2)
+                ref = self.view(*at, None)
+                self.sibs.append(Send(ref, ref, sib, self.view(*at, None, oc)))
+
         def stage5(self):
             for s in self.sibs:
                 s.wait()
@@ -168,11 +176,11 @@
         return kvbuf.at[c, aa, bb, pl.ds((0, 128)[part], (128, 144)[part])]
 
     def w_view(first, x_first):
-        def view(aa, bb, part):
+        def view(aa, bb, part, core=c):
             xx, yy = (aa, bb) if x_first else (bb, aa)
             if part is None:
-                return wbuf.at[xx, yy, c, :, pl.ds(first, 512)]
-            return wbuf.at[xx, yy, c, :, pl.ds(first + 256 * part, 256)]
+                return wbuf.at[xx, yy, core, :, pl.ds(first, 512)]
+            return wbuf.at[xx, yy, core, :, pl.ds(first + 256 * part, 256)]
 
         return view
 
@@ -235,17 +243,20 @@
     gather_w1.stage0()
     loads[2].wait()
 
-    doc_row = lax.broadcasted_iota(jnp.int32, (HEAD, T), 0).astype(F32)
-    token = lax.broadcasted_iota(jnp.int32, (HEAD, T), 1).astype(F32)
-    own_doc = jnp.where(token >= below1, 1.0, 0.0) + jnp.where(token >= below2, 1.0, 0.0)
-    one_hot = jnp.where(own_doc == doc_row, 1.0, 0.0).astype(BF16)
+    rows = lax.broadcasted_iota(jnp.int32, (T, 128), 0).astype(F32)
+    lanes = lax.broadcasted_iota(jnp.int32, (T, 128), 1).astype(F32)
+
+    def doc_of(n1, n2):
+        return jnp.where(rows >= n1, 1.0, 0.0) + jnp.where(rows >= n2, 1.0, 0.0)
+
+    one_hot = jnp.where(doc_of(below1, below2) == lanes, 1.0, 0.0).astype(BF16)
     for h in range(8):
         at = pl.ds((h % 4) * T, T)
-        qa[h // 4, 0:HEAD, at] = jnp.transpose(q_ref[:, h * HEAD : (h + 1) * HEAD])
-        qa[h // 4, HEAD : 2 * HEAD, at] = one_hot
-
-    key_row = lax.broadcasted_iota(jnp.int32, (T, HEAD), 0).astype(F32)
-    doc_lane = lax.broadcasted_iota(jnp.int32, (T, HEAD), 1).astype(F32)
+        qa[h // 4, at, 0:HEAD] = q_ref[:, h * HEAD : (h + 1) * HEAD]
+        qa[h // 4, at, HEAD : 2 * HEAD] = one_hot
+
+    doc_id = lax.broadcasted_iota(jnp.int32, (16, T), 0).astype(F32)
+    key_id = lax.broadcasted_iota(jnp.int32, (16, T), 1).astype(F32)
 
     def blocks(tt):
         xx, yy = lax.div(tt, 4), lax.rem(tt, 4)
@@ -255,51 +266,52 @@
         sides = []
         for block in blocks(tt):
             strip = block[T : T + 16, 0:HEAD].astype(F32)
-            doc = jnp.where(key_row >= strip[0:1, :], 1.0, 0.0) + jnp.where(key_row >= strip[8:9, :], 1.0, 0.0)
-            bias = jnp.where(doc == doc_lane, 0.0, -BIG).astype(BF16)
-            sides.append(jnp.concatenate([block[0:T, 0:HEAD], bias], axis=1))
-        return jnp.concatenate(sides, axis=0)
-
-    ones = jnp.ones((16, 2 * T), BF16)
+            doc = jnp.where(key_id >= strip[0:1, 0:1], 1.0, 0.0) + jnp.where(key_id >= strip[8:9, 0:1], 1.0, 0.0)
+            bias = jnp.where(doc == doc_id, 0.0, -BIG).astype(BF16)
+            rest = jnp.zeros((HEAD - 16, T), BF16)
+            sides.append(jnp.concatenate([jnp.transpose(block[0:T, 0:HEAD]), bias, rest], axis=0))
+        return jnp.concatenate(sides, axis=1)
+
+    ones = jnp.ones((2 * T, HEAD), BF16)
 
     def wide(v, n):
         return jnp.concatenate([v] * n, axis=1)
 
     def values_of(tt):
-        v = jnp.concatenate([jnp.transpose(block[0:T, HEAD : 2 * HEAD]) for block in blocks(tt)], axis=1)
-        return jnp.concatenate([v, ones], axis=0)
+        v = jnp.concatenate([block[0:T, HEAD : 2 * HEAD] for block in blocks(tt)], axis=0)
+        return jnp.concatenate([v, ones], axis=1)
 
     def soften(group, scores, weights, own):
         factors = []
         for piece in range(8):
             at = slice(piece * 128, (piece + 1) * 128)
-            s = scores[:, at]
+            s = scores[at, :]
             if own:
-                row = lax.broadcasted_iota(jnp.int32, (2 * T, 128), 0)
-                col = lax.broadcasted_iota(jnp.int32, (2 * T, 128), 1) + (piece % 2) * 128
-                s = jnp.where(row <= col + c * T, s, -2.0 * BIG)
-                m = jnp.max(s, axis=0, keepdims=True)
+                row = lax.broadcasted_iota(jnp.int32, (128, 2 * T), 0) + (piece % 2) * 128
+                col = lax.broadcasted_iota(jnp.int32, (128, 2 * T), 1)
+                s = jnp.where(col <= row + c * T, s, -2.0 * BIG)
+                m = jnp.broadcast_to(jnp.max(s, axis=1, keepdims=True), (128, 128))
             else:
-                m_old = m_ref[group, 0:1, at]
-                m = jnp.maximum(m_old, jnp.max(s, axis=0, keepdims=True))
+                m_old = m_ref[group, at, :]
+                m = jnp.maximum(m_old, jnp.max(s, axis=1, keepdims=True))
                 factors.append(jnp.exp2((m_old - m) * EXP_SCALE))
-            weights[:, at] = jnp.exp2(((s - m) * EXP_SCALE).astype(BF16))
-            m_ref[group, 0:1, at] = m
+            weights[at, :] = jnp.exp2(((s - wide(m, 4)) * EXP_SCALE).astype(BF16))
+            m_ref[group, at, :] = m
         return factors
 
     def gather_values(group, weights, values, factors):
-        update = dot(values, weights[...])
+        update = dot(weights[...], values)
         if not factors:
             acc_ref[group] = update
             return
         for piece, factor in enumerate(factors):
             at = slice(piece * 128, (piece + 1) * 128)
-            acc_ref[group, :, at] = acc_ref[group, :, at] * factor + update[:, at]
+            acc_ref[group, at, :] = acc_ref[group, at, :] * wide(factor, 2) + update[at, :]
 
     def attend_chip(tt, own):
         keys, values = keys_of(tt), values_of(tt)
-        s_a = dot(keys, qa[0])
-        s_b = dot(keys, qa[1])
+        s_a = dot(qa[0], keys)
+        s_b = dot(qa[1], keys)
         factors_a = soften(0, s_a, pa_ref, own)
         gather_values(0, pa_ref, values, factors_a)
         factors_b = soften(1, s_b, pb_ref, own)
@@ -327,9 +339,9 @@
 
     def finish():
         for h in range(8):
-            at = pl.ds((h % 4) * T, T)
-            out = acc_ref[h // 4, 0:HEAD, at] / acc_ref[h // 4, HEAD : HEAD + 1, at]
-            to_ref[128 : 128 + T, h * HEAD : (h + 1) * HEAD] = jnp.transpose(out.astype(BF16))
+            acc = acc_ref[h // 4, pl.ds((h % 4) * T, T), :]
+            out = (acc[:, 0:HEAD] / acc[:, HEAD : 2 * HEAD]).astype(BF16)
+            to_ref[128 : 128 + T, h * HEAD : (h + 1) * HEAD] = out
         last = Send(
             to_ref.at[pl.ds(128 + T - HALO, HALO)], to_ref.at[pl.ds(128 - HALO, HALO)],
             {"seq": lax.rem(i + 1, 32)},
@@ -385,39 +397,63 @@
         gather.to_sib(-1)
         gather.to_sib(1)
     attend(far, 0, 3)
-    gather_w0.stage4()
-    gather_w1.stage4()
-    attend(far, 3, 7)
+    attend(far, 3, 5)
+    gather_w0.stage4_by_shard()
+    gather_w1.stage4_by_shard()
+    attend(far, 5, 7)
     gathered = len(sent)
     halos = finish()
-    gather_w0.stage5()
-    gather_w1.stage5()
-
-    def predict(piece, carry):
+
+    def predict_rows(xx, cols):
+        rows = pl.ds(pl.multiple_of(xx * 896, 128), 896)
+        return dot(normed[:, rows], wbuf[xx, :, :, :, cols].reshape(896, 256))
+
+    def predict_second(rows, fresh):
+        def step(piece, carry):
+            cols = pl.ds(pl.multiple_of(512 + piece * 256, 256), 256)
+            total = jnp.zeros((T, 256), F32) if fresh else p_ref[:, cols]
+            for d in rows:
+                total = total + predict_rows(mod4(x + d), cols)
+            p_ref[:, cols] = total
+            return carry
+
+        lax.fori_loop(0, 2, step, 0)
+
+    def predict_first(piece, carry):
         cols = pl.ds(pl.multiple_of(piece * 256, 256), 256)
         total = jnp.zeros((T, 256), F32)
         for xx in range(4):
-            total = total + dot(normed[:, xx * 896 : (xx + 1) * 896], wbuf[xx, :, :, :, cols].reshape(896, 256))
+            total = total + predict_rows(xx, cols)
         p_ref[:, cols] = total
         return carry
 
-    lax.fori_loop(0, 4, predict, 0)
+    inner = [jnp.zeros((T, 128), F32)]
+    send_r = []
+
+    def residual(half):
+        for piece in (2 * half, 2 * half + 1):
+            cols = slice(piece * 256, (piece + 1) * 256)
+            target = dot(select, to_ref[:, cols]) * wide(inverse_count, 2)
+            prediction = p_ref[:, cols]
+            value = (prediction - target).astype(BF16)
+            r_ref[:, cols] = value
+            product = value.astype(F32) * prediction
+            inner[0] = inner[0] + product[:, 0:128] + product[:, 128:256]
+        cols = pl.ds(half * 512, 512)
+        send_r.append(Send(r_ref.at[:, cols], rsib.at[:, cols], sib))
+
+    for s in gather_w1.sibs[:3]:
+        s.wait()
+    predict_second((0, 1, -1), True)
+    for s in gather_w0.sibs + gather_w1.sibs[3:]:
+        s.wait()
+    lax.fori_loop(0, 2, predict_first, 0)
     for s in halos:
         s.wait()
-
-    inner = jnp.zeros((T, 128), F32)
-    send_r = []
-    for piece in range(4):
-        cols = slice(piece * 256, (piece + 1) * 256)
-        target = dot(select, to_ref[:, cols]) * wide(inverse_count, 2)
-        prediction = p_ref[:, cols]
-        residual = (prediction - target).astype(BF16)
-        r_ref[:, cols] = residual
-        product = residual.astype(F32) * prediction
-        inner = inner + product[:, 0:128] + product[:, 128:256]
-        if piece % 2 == 1:
-            half = pl.ds((piece - 1) * 256, 512)
-            send_r.append(Send(r_ref.at[:, half], rsib.at[:, half], sib))
+    residual(0)
+    predict_second((2,), False)
+    residual(1)
+    inner = inner[0]
     inner = jnp.broadcast_to(jnp.sum(inner, axis=1, keepdims=True), (T, 128))
     in_own[...] = jnp.transpose(inner)[0:8, :]
     inners = [Send(in_own, in_all.at[d], {"tp": lax.rem(z + d, 8)}) for d in range(1, 8)]
@@ -629,11 +665,11 @@
         vm((T, WIDE)),
         vm((2, 4, 4, T + 16, 2 * HEAD)),
         vm((4, 4, 2, 112, FEAT)),
-        vm((2, 2 * HEAD, 4 * T)),
-        vm((2, 8, 4 * T), F32),
-        vm((2, HEAD + 16, 4 * T), F32),
-        vm((2 * T, 4 * T)),
-        vm((2 * T, 4 * T)),
+        vm((2, 4 * T, 2 * HEAD)),
+        vm((2, 4 * T, 128), F32),
+        vm((2, 4 * T, 2 * HEAD), F32),
+        vm((4 * T, 2 * T)),
+        vm((4 * T, 2 * T)),
         vm((512, FEAT)),
         vm((T, WIDE)),
         vm((4, 4, 2, 112, T)),

time: 96.5 us -> 93.5 us (0.969)
  Pallas kernels: 95.5 us -> 92.6 us
    pallas_call x1, Pallas kernels: 93.5 us -> 90.6 us  [body(): pl.pallas_call(kernel, out_shape=(jax.ShapeDtypeStruct((112, FEAT), F32),...]
where the time goes in v6:
time: 93.5 us; the launch traced here: 93.4 us
  Pallas kernels  92.6 us (99%)
    pallas_call x1, Pallas kernels, body(): pl.pallas_call(kernel, out_shape=(jax.ShapeDtypeStruct((112, FEAT), F32),...  90.6 us
    pallas_call x1, Pallas kernels, body(): pl.pallas_call(deliver, out_shape=(jax.ShapeDtypeStruct((112, FEAT), F32)...  1.97 us

profile of v6, /device:TPU:32, one launch (start us, length us, event | category | flops | bytes accessed | tf_op | source)
XLA Modules:
  0.0 93.4 jit_solution(10438288180627669793)
XLA Ops:
  0.6 90.6 %shard_map.104 = (f32[112,1024]{1,0:T(8,128)}, f32[448,256]{1,0:T(8,128)}) custom-call(bf16[256,1024]{1,0:T(8,128)(2,1)} %q_hbm.1, bf16[256,128]{1,0:T(8,128)(2,1)} %k_ref.1, bf16[256,128]{1,0:T(8,128)(2,1)} %v_ref.1, s32[1,256]{1,0:T(1,128)} %bitcast.6, bf16[256,3584]{1,0:T(8,128)(2,1)} %sh_hbm.1, f32[28,128]{1,0:T(8,128)} %bitcast.5, ...), custom_call_target="tpu_custom_call" | custom-call | tf_op jit(solution)/shard_map/pallas_call | solution.py:698
  91.2 2.0 %shard_map.105 = (f32[112,1024]{1,0:T(8,128)}, f32[448,256]{1,0:T(8,128)}) custom-call(f32[112,1024]{1,0:T(8,128)} %get-tuple-element.6.gp_in, f32[448,256]{1,0:T(8,128)} %get-tuple-element.7.gh_in), custom_call_target="tpu_custom_call" | custom-call | tf_op jit(solution)/shard_map/pallas_call | solution.py:711

commit v7 on v6

--- a/solution.py
+++ b/solution.py
@@ -236,11 +236,6 @@
         return carry
 
     lax.fori_loop(0, 1, norm_piece, 0)
-    gather_kv.stage1()
-    near_shared = [share(1, 0), share(-1, 0), share(0, 1), share(0, -1)]
-    loads[1].wait()
-    gather_w0.stage0()
-    gather_w1.stage0()
     loads[2].wait()
 
     rows = lax.broadcasted_iota(jnp.int32, (T, 128), 0).astype(F32)
@@ -365,42 +360,47 @@
     begin, end = wide(span_start, 4), wide(span_start + span_count, 4)
     select = jnp.where((row_id >= begin) & (row_id < end), 1.0, 0.0).astype(BF16)
 
+    gather_kv.stage1()
+    near_shared = [share(1, 0), share(-1, 0), share(0, 1), share(0, -1)]
+    shared[0].wait()
+    attend_chip(t, True)
     gather_kv.stage2()
     far_shared = [share(2, 0)]
-    shared[0].wait()
-    attend_chip(t, True)
+    loads[1].wait()
+    gather_w0.stage0()
+    gather_w1.stage0()
     gather_kv.stage2b()
     near_shared += [share(da, db) for da in (1, -1) for db in (1, -1)]
     lax.fori_loop(1, 4, norm_piece, 0)
     send_nt = Send(nt_ref.at[:, :, oc], nsib, sib)
+    gather_kv.stage3()
+    far_shared += [share(2, 1), share(2, -1)]
     for s in near_shared:
         s.wait()
+    attend(near, 0, 2)
     gather_w0.stage1()
     gather_w1.stage1()
-    attend(near, 0, 2)
-    gather_kv.stage3()
-    far_shared += [share(2, 1), share(2, -1)]
     attend(near, 2, 4)
+    gather_kv.stage4()
+    attend(near, 4, 7)
     for gather in (gather_w0, gather_w1):
         gather.stage2()
         gather.to_sib(0)
-    attend(near, 4, 6)
-    gather_kv.stage4()
-    gather_w0.stage2b()
-    gather_w1.stage2b()
-    attend(near, 6, 8)
+    attend(near, 7, 8)
     for s in far_shared:
         s.wait()
     gather_kv.stage5()
+    gather_w0.stage2b()
+    gather_w1.stage2b()
+    attend(far, 0, 1)
     for gather in (gather_w0, gather_w1):
         gather.stage3()
         gather.to_sib(-1)
         gather.to_sib(1)
-    attend(far, 0, 3)
-    attend(far, 3, 5)
+    attend(far, 1, 4)
     gather_w0.stage4_by_shard()
     gather_w1.stage4_by_shard()
-    attend(far, 5, 7)
+    attend(far, 4, 7)
     gathered = len(sent)
     halos = finish()
 

time: 93.5 us -> 94.4 us (level)
  no operation moved by 1% of the time
where the time goes in v7:
time: 94.4 us; the launch traced here: 94.2 us
  Pallas kernels  93.4 us (99%)
    pallas_call x1, Pallas kernels, body(): pl.pallas_call(kernel, out_shape=(jax.ShapeDtypeStruct((112, FEAT), F32),...  91.5 us
    pallas_call x1, Pallas kernels, body(): pl.pallas_call(deliver, out_shape=(jax.ShapeDtypeStruct((112, FEAT), F32)...  1.97 us

profile of v7, /device:TPU:32, one launch (start us, length us, event | category | flops | bytes accessed | tf_op | source)
XLA Modules:
  0.0 94.2 jit_solution(8343076781426738716)
XLA Ops:
  0.6 91.5 %shard_map.104 = (f32[112,1024]{1,0:T(8,128)}, f32[448,256]{1,0:T(8,128)}) custom-call(bf16[256,1024]{1,0:T(8,128)(2,1)} %q_hbm.1, bf16[256,128]{1,0:T(8,128)(2,1)} %k_ref.1, bf16[256,128]{1,0:T(8,128)(2,1)} %v_ref.1, s32[1,256]{1,0:T(1,128)} %bitcast.6, bf16[256,3584]{1,0:T(8,128)(2,1)} %sh_hbm.1, f32[28,128]{1,0:T(8,128)} %bitcast.5, ...), custom_call_target="tpu_custom_call" | custom-call | tf_op jit(solution)/shard_map/pallas_call | solution.py:698
  92.1 2.0 %shard_map.105 = (f32[112,1024]{1,0:T(8,128)}, f32[448,256]{1,0:T(8,128)}) custom-call(f32[112,1024]{1,0:T(8,128)} %get-tuple-element.6.gp_in, f32[448,256]{1,0:T(8,128)} %get-tuple-element.7.gh_in), custom_call_target="tpu_custom_call" | custom-call | tf_op jit(solution)/shard_map/pallas_call | solution.py:711
